TPU v7x, 256 devices: a whole 4x4x8 slice. The times are simulated.
256 devices in a mesh: inner: 8 (over y, z_lo), outer: 8 (over z_hi, core), tensor: 4 (over x).
Axes of the slice: x: 4, y: 4, z: 8 (z_hi: 4, z_lo: 2; z = z_hi * 2 + z_lo), core: 2. Of those that a mesh axis runs over, the one named last changes fastest.
Arguments:
- query_matrix: bfloat16 [8192, 4096], P(('inner', 'outer'), 'tensor'), may hold values from -6 to 6
- key_matrix: bfloat16 [8192, 512], P(('inner', 'outer'), 'tensor'), may hold values from -6 to 6
- value_matrix: bfloat16 [8192, 512], P(('inner', 'outer'), 'tensor'), may hold values from -12 to 12
- segment_ids: int32 [8192], replicated, may hold values from 0 to 7, never falling along the last dimension, each value on 1 to 4096 neighbouring positions
- block_order: int32 [128], replicated, may hold values from 0 to 127, each once
- out_weight: bfloat16 [4096, 4096], P('tensor'), may hold values from -0.09375 to 0.09375
- d_attended: bfloat16 [8192, 4096], P(('inner', 'outer', 'tensor')), may hold values from -6 to 6
Outputs:
- attended: bfloat16 [8192, 4096], P(('inner', 'outer'), 'tensor')
- d_queries: bfloat16 [8192, 4096], P(('inner', 'outer'), 'tensor')
- key_gradient: bfloat16 [8192, 512], P(('inner', 'outer'), 'tensor')
- value_gradient: bfloat16 [8192, 512], P(('inner', 'outer'), 'tensor')
Inputs may be any that keep to these rules, and one draw needn't show every extreme that they name: `segment_ids`: never falls along the sequence position; each of the 8 documents holds one or more positions, at most half of 8192, and one holds exactly half of 8192. `block_order`: each of the 128 blocks exactly once.
All inputs are finite; a program needn't handle non-finite values.
Results may differ from a plain program's by a relative error of at most 0.019.
Values may be sent and summed in bfloat16 or wider, within the bound.
A program may use at most 128 MiB of HBM per device.

v0:
```python
import math

import jax
import jax.numpy as jnp
from jax import lax
from jax.sharding import PartitionSpec as P

HEAD_FEATURES = 128


def token_places(segment_ids, block_order, row_count, span_rows):
    row_ids = jnp.arange(row_count, dtype=jnp.int32)
    slot_ids = row_ids // span_rows
    slot_table = jnp.arange(block_order.shape[0], dtype=jnp.int32)
    span_ids = jnp.sum(
        jnp.where(slot_ids[:, None] == slot_table[None, :], block_order[None, :], 0), axis=1
    )
    places = span_ids * span_rows + row_ids % span_rows
    return (places, jnp.take(segment_ids, places))


def shards(
    query_matrix, key_matrix, value_matrix, segment_ids, block_order, out_weight, d_attended
):
    row_count = query_matrix.shape[0]
    span_rows = row_count // 2
    kv_width = key_matrix.shape[1]
    kv_heads = kv_width // HEAD_FEATURES
    group_size = query_matrix.shape[1] // kv_width
    softmax_scale = 1.0 / math.sqrt(HEAD_FEATURES)
    seq_index = lax.axis_index(("inner", "outer"))
    paired = jnp.concatenate([key_matrix, value_matrix], axis=1)
    gathered = lax.all_gather(paired, ("inner", "outer"), axis=0, tiled=True)
    total_rows = gathered.shape[0]
    places, documents = token_places(segment_ids, block_order, total_rows, span_rows)
    own_start = seq_index * row_count
    own_places = lax.dynamic_slice_in_dim(places, own_start, row_count, 0)
    own_docs = lax.dynamic_slice_in_dim(documents, own_start, row_count, 0)
    visible = (
        (places[:, None] <= own_places[None, :]) & (documents[:, None] == own_docs[None, :])
    )[:, None, :]
    heads_of_keys = gathered[:, :kv_width].reshape(total_rows, kv_heads, HEAD_FEATURES)
    heads_of_values = gathered[:, kv_width:].reshape(total_rows, kv_heads, HEAD_FEATURES)
    attention_gradient = lax.dot_general(
        lax.all_gather(d_attended, "tensor", axis=0, tiled=True),
        out_weight,
        (((1,), (1,)), ((), ())),
        preferred_element_type=jnp.float32,
    ).astype(jnp.bfloat16)
    query_by_head = jnp.transpose(
        query_matrix.reshape(row_count, kv_heads, group_size, HEAD_FEATURES), (2, 0, 1, 3)
    )
    grad_by_head = jnp.transpose(
        attention_gradient.reshape(row_count, kv_heads, group_size, HEAD_FEATURES), (2, 0, 1, 3)
    )

    def head_pass(query_head, grad_head):
        scores = (
            jnp.einsum(
                "kad,qad->kaq", heads_of_keys, query_head, preferred_element_type=jnp.float32
            )
            * softmax_scale
        )
        scores = jnp.where(visible, scores, -1e30)
        row_max = jnp.max(scores, axis=0)
        exponent = jnp.where(visible, jnp.exp(scores - row_max), 0.0)
        row_sum = jnp.sum(exponent, axis=0)
        weights = exponent.astype(jnp.bfloat16)
        mixed_values = jnp.einsum(
            "kaq,kad->qad", weights, heads_of_values, preferred_element_type=jnp.float32
        )
        attended_head = (mixed_values / jnp.transpose(row_sum, (1, 0))[..., None]).astype(
            jnp.bfloat16
        )
        row_delta = jnp.einsum(
            "qad,qad->aq", grad_head, attended_head, preferred_element_type=jnp.float32
        )
        normed = weights.astype(jnp.float32) / row_sum
        prob_b = normed.astype(jnp.bfloat16)
        d_prob = jnp.einsum(
            "qad,kad->kaq", grad_head, heads_of_values, preferred_element_type=jnp.float32
        )
        d_score = (normed * (d_prob - row_delta)).astype(jnp.bfloat16)
        dq_head = jnp.einsum(
            "kaq,kad->qad", d_score, heads_of_keys, preferred_element_type=jnp.float32
        )
        d_query = (dq_head * softmax_scale).astype(jnp.bfloat16)
        return (attended_head, d_query, prob_b, d_score)

    def with_sums(carried, heads):
        key_sum, value_sum = carried
        query_head, grad_head = heads
        attended_head, d_query, prob_b, d_score = head_pass(query_head, grad_head)
        key_sum = key_sum + jnp.einsum(
            "kaq,qad->kad", d_score, query_head, preferred_element_type=jnp.float32
        )
        value_sum = value_sum + jnp.einsum(
            "kaq,qad->kad", prob_b, grad_head, preferred_element_type=jnp.float32
        )
        return ((key_sum, value_sum), (attended_head, d_query))

    head_inputs = (query_by_head, grad_by_head)
    zeroed_sums = jnp.zeros((total_rows, kv_heads, HEAD_FEATURES), jnp.float32)
    term_sums, outputs = lax.scan(with_sums, (zeroed_sums, zeroed_sums), head_inputs)
    attended_stack, dq_stack = outputs
    all_terms = jnp.concatenate(
        [term_sums[0].reshape(total_rows, kv_width), term_sums[1].reshape(total_rows, kv_width)],
        axis=1,
    )
    gradient_sums = lax.psum_scatter(all_terms, ("inner", "outer"), scatter_dimension=0, tiled=True)
    attended = jnp.transpose(attended_stack, (1, 2, 0, 3)).reshape(row_count, query_matrix.shape[1])
    d_queries = jnp.transpose(dq_stack, (1, 2, 0, 3)).reshape(row_count, query_matrix.shape[1])
    key_gradient = (gradient_sums[:, :kv_width] * softmax_scale).astype(jnp.bfloat16)
    value_gradient = gradient_sums[:, kv_width:].astype(jnp.bfloat16)
    return (attended, d_queries, key_gradient, value_gradient)


def solution(mesh):
    return jax.shard_map(
        shards,
        mesh=mesh,
        in_specs=(
            P(("inner", "outer"), "tensor"),
            P(("inner", "outer"), "tensor"),
            P(("inner", "outer"), "tensor"),
            P(),
            P(),
            P("tensor", None),
            P(("inner", "outer", "tensor"), None),
        ),
        out_specs=(
            P(("inner", "outer"), "tensor"),
            P(("inner", "outer"), "tensor"),
            P(("inner", "outer"), "tensor"),
            P(("inner", "outer"), "tensor"),
        ),
        check_vma=False,
    )
```

profile of v0, /device:TPU:32, one launch (start us, length us, event | category | flops | bytes accessed | tf_op | source)
XLA Modules:
  0.0 579.2 jit_solution(16569772296996533132)
XLA Ops:
  9.5 3.2 select_reduce_fusion
  12.8 45.5 %gather_fusion = s32[8192]{0:T(1024)S(1)} fusion(s32[8192]{0:T(1024)S(1)} %copy-done, s32[8192]{0:T(1024)S(1)} %broadcast_clamp_fusion), kind=kCustom, calls=%fused_computation | custom fusion | bytes 98304 | tf_op jit(solution)/shard_map/jit(_take)/gather | solution.py:19
  58.8 6.7 %fusion.63 = bf16[16,8,8,128]{3,1,2,0:T(8,128)(2,1)S(1)} fusion(bf16[128,4096]{1,0:T(8,128)(2,1)} %all-gather.5.cloned.1.call-done, bf16[1024,4096]{1,0:T(8,128)(2,1)} %param.14), kind=kOutput, calls=%fused_computation.57 | convolution fusion | flops 1073872896 | bytes 9699328 | tf_op jit(solution)/shard_map/dot_general | solution.py:44
  65.5 92.2 %all-gather.3.cloned.1.call-done = bf16[8192,256]{1,0:T(8,128)(2,1)} async-done(((bf16[128,256]{1,0:T(8,128)(2,1)}), bf16[8192,256]{1,0:T(8,128)(2,1)}) %all-gather.3.cloned.1.call-update) | async-done | bytes 4194320 | tf_op jit(solution)/shard_map/all_gather | solution.py:33
  157.7 3.8 slice_bitcast_fusion
  161.6 122.3 %while.17 = (s32[]{:T(128)}, f32[8192,1,128]{0,2,1:T(8,128)}, f32[8192,1,128]{0,2,1:T(8,128)}, bf16[8,128,1,128]{3,1,2,0:T(8,128)(2,1)S(1)}, bf16[8,128,1,128]{3...) while((s32[]{:T(128)}, f32[8192,1,128]{0,2,1:T(8,128)}, ...), condition=%wide.region_4.5_spmd.clone, body=%wide.region_1.4_spmd.clone.sunk | while | flops 1636957824 | bytes 124164416 | solution.py:104
  161.6 3.1 fusion.102
  174.9 1.9 copy-done.2
  176.8 3.1 fusion.102
  190.2 1.9 copy-done.2
  192.1 3.1 fusion.102
  207.4 3.1 fusion.102
  220.8 1.9 copy-done.2
  222.7 3.1 fusion.102
  238.0 3.1 fusion.102
  251.3 1.9 copy-done.2
  253.3 3.1 fusion.102
  266.6 1.9 copy-done.2
  268.6 3.1 fusion.102
  281.9 1.9 copy-done.2
  283.8 5.6 copy.28
  289.4 5.6 copy.29
  295.0 7.2 %pad_maximum_fusion = f32[8192,256]{1,0:T(8,128)} fusion(f32[8192,128]{1,0:T(8,128)} %bitcast.188, f32[8192,128]{1,0:T(8,128)} %bitcast.187), kind=kLoop, calls=%fused_computation.51 | loop fusion | flops 2097152 | bytes 16777216 | tf_op jit(solution)/shard_map/concatenate | solution.py:106
  303.5 266.3 %reduce-scatter.2.cloned.1.call-done = f32[128,256]{1,0:T(8,128)} async-done(((f32[8192,256]{1,0:T(8,128)}), f32[128,256]{1,0:T(8,128)}) %reduce-scatter.2.cloned.1.call-update) | async-done | bytes 131088 | tf_op jit(solution)/shard_map/reduce_scatter | solution.py:110
  (161 shorter events, 92.2 us)
Async XLA Ops:
  7.2 5.7 copy-start
  7.2 51.6 %all-gather.5.cloned.1.call-start = ((), (), s32[]{:S(2)}) async-start(), calls=%async_computation.2 | async-start | bytes 1310720 | tf_op jit(solution)/shard_map/all_gather | solution.py:45
  7.9 149.8 %all-gather.3.cloned.1.call-start = ((), (), s32[]{:S(2)}) async-start(), calls=%async_computation.1 | async-start | bytes 4259840 | tf_op jit(solution)/shard_map/all_gather | solution.py:33
  9.4 560.4 %reduce-scatter.2.cloned.1.call-start = ((), (), s32[]{:S(2)}) async-start(), calls=%async_computation.3 | async-start | bytes 8519680 | tf_op jit(solution)/shard_map/reduce_scatter | solution.py:110
  12.8 45.7 %copy-start.6 = (bf16[128,1024]{1,0:T(8,128)(2,1)S(1)}, bf16[128,1024]{1,0:T(8,128)(2,1)}, u32[]{:S(2)}) copy-start(bf16[128,1024]{1,0:T(8,128)(2,1)} %param.9) | copy-start | bytes 786436
  168.6 2.2 copy-start.4
  170.7 2.2 copy-start.1
  172.9 2.0 copy-start.5
  183.8 2.2 copy-start.4
  186.0 2.2 copy-start.1
  199.1 2.2 copy-start.4
  201.3 2.2 copy-start.1
  214.4 2.2 copy-start.4
  216.6 2.2 copy-start.1
  229.7 2.2 copy-start.4
  231.9 2.2 copy-start.1
  245.0 2.2 copy-start.4
  247.2 2.2 copy-start.1
  249.4 2.0 copy-start.5
  260.3 2.2 copy-start.4
  262.5 2.2 copy-start.1
  275.6 2.2 copy-start.4
  277.7 2.2 copy-start.1
  279.9 2.0 copy-start.5
  (21 other events, 38.1 us)
Sparse Core Ops, SparseCore 0:
  9.8 29.0 all-gather.4
  41.4 116.2 all-gather.2
  302.4 267.3 reduce-scatter.1
where the time goes:
time: 589 us; the launch traced here: 579 us
  waiting for transfers between devices  359 us (61%)
  local copies, waits for them, and re-layouts  104 us (18%)
  matrix products  76.4 us (13%)
  other arithmetic  25.2 us (4%)
  between operations  13.9 us (2%)
    reduce_scatter x1, waiting for transfers between devices, shards(): lax.psum_scatter(all_terms, ('inner', 'outer'), scatter_dimension=0, tile...  266 us
    all_gather x1, waiting for transfers between devices, shards(): gathered = lax.all_gather(paired, ('inner', 'outer'), axis=0, tiled=True)  92.2 us
    gather x1, local copies, waits for them, and re-layouts, token_places(): return (places, jnp.take(segment_ids, places))  45.5 us
    while x80, local copies, waits for them, and re-layouts  40.4 us
    dot_general x8, matrix products, head_pass(): jnp.einsum('kad,qad->kaq', heads_of_keys, query_head, preferred_element_t...  25 us
    dot_general x8, matrix products, with_sums(): jnp.einsum('kaq,qad->kad', prob_b, grad_head, preferred_element_type=jnp....  13.1 us
    dot_general x8, matrix products, with_sums(): jnp.einsum('kaq,qad->kad', d_score, query_head, preferred_element_type=jn...  13 us
  transfers between devices with their start and end apart: 3, of which 2 were waited for; matrix products, arithmetic and copies ran while one was open for 10% of the time, Pallas kernels for 0%

commit v1 on v0

v1 whole, which is shorter than its diff:
```python
import functools
import math

import jax
import jax.numpy as jnp
from jax import lax
from jax.experimental import pallas as pl
from jax.experimental.pallas import tpu as pltpu
from jax.sharding import PartitionSpec as P

D = 128
HEADS = 8
ROWS = 128
SPAN = 64
SPANS = 128
TOKENS = 8192
QROWS = SPAN * HEADS
TILE_SPANS = 8
TILE = TILE_SPANS * SPAN
MAX_TILES = 65 // TILE_SPANS + 1
SCALE = 1.0 / math.sqrt(D)
EXP2_SCALE = SCALE * math.log2(math.e)
F32 = jnp.float32
BF16 = jnp.bfloat16
MESH = pl.DeviceIdType.MESH
VMEM = pl.BlockSpec(memory_space=pltpu.VMEM)
SMEM = pl.BlockSpec(memory_space=pltpu.SMEM)
ANY = pl.BlockSpec(memory_space=pl.ANY)
LIMIT = 56 * 1024 * 1024
PIECES = (4, 2, 4, 2, ROWS, 2 * D)


class Place:
    def __init__(self):
        inner, outer = lax.axis_index("inner"), lax.axis_index("outer")
        self.x = lax.axis_index("tensor")
        self.y = lax.div(inner, 2)
        self.core = lax.rem(outer, 2)
        z = lax.div(outer, 2) * 2 + lax.rem(inner, 2)
        self.ys = [lax.rem(self.y + s, 4) for s in range(4)]
        self.xs = [lax.rem(self.x + s, 4) for s in range(4)]
        zs = [lax.rem(z + s, 8) for s in range(8)]
        self.zs = [(at, lax.rem(at, 2), lax.div(at, 2)) for at in zs]
        self.z = self.zs[0]

    def dy(self, step):
        return self.ys[step % 4]

    def dz(self, step):
        return self.zs[step % 8]

    def dx(self, step):
        return self.xs[step % 4]

    def device(self, y=None, z=None, core=None, x=None):
        y = self.y if y is None else y
        z = self.z if z is None else z
        core = self.core if core is None else core
        x = self.x if x is None else x
        return (y * 2 + z[1], z[2] * 2 + core, x)

    def greet(self, devices):
        barrier = pltpu.get_barrier_semaphore()
        for device in devices:
            pl.semaphore_signal(barrier, inc=1, device_id=device, device_id_type=MESH)
        pl.semaphore_wait(barrier, len(devices))


class Sends:
    def __init__(self, sems):
        self.sems, self.copies = sems, []

    def __call__(self, src, dst, recv_sem, device):
        copy = pltpu.make_async_remote_copy(
            src_ref=src, dst_ref=dst, send_sem=self.sems.at[len(self.copies)],
            recv_sem=recv_sem, device_id=device, device_id_type=MESH,
        )
        copy.start()
        self.copies.append(copy)

    def wait(self):
        for copy in self.copies:
            copy.wait_send()
        self.copies = []


def arrived(ref, send_sem, recv_sem, device):
    pltpu.make_async_remote_copy(
        src_ref=ref, dst_ref=ref, send_sem=send_sem, recv_sem=recv_sem,
        device_id=device, device_id_type=MESH,
    ).wait_recv()


def piece(ref, y, z, *core):
    return ref.at[(y, z[1], z[2]) + core]


def gather_kernel(
    k_ref, v_ref, da_ref, w_ref, kv_ref, g_ref,
    own, da_all, w_all, local_sem, send_sem, recv_sem, mate_send, mate_recv, x_send, x_recv,
):
    me = Place()
    y, z, x = me.y, me.z, me.x
    w_copy = pltpu.make_async_copy(w_ref, w_all, local_sem.at[0])
    w_copy.start()
    own[:, :D] = k_ref[...]
    own[:, D:] = v_ref[...]
    own_copy = pltpu.make_async_copy(own, piece(kv_ref, y, z, me.core), local_sem.at[1])
    own_copy.start()
    da_all[x] = da_ref[...]
    mate = me.device(core=1 - me.core)
    me.greet(
        [mate]
        + [me.device(y=me.dy(s)) for s in (1, -1, 2)]
        + [me.device(z=me.dz(s)) for s in (1, -1)]
        + [me.device(x=me.dx(s)) for s in (1, -1)]
    )
    up_x, down_x = me.device(x=me.dx(1)), me.device(x=me.dx(-1))
    half = da_ref.shape[1] // 2
    x_sends = Sends(x_send)

    def x_start():
        x_sends(da_ref, da_all.at[x], x_recv.at[0], up_x)
        x_sends(da_ref, da_all.at[x], x_recv.at[1], down_x)

    def x_middle():
        low, high = me.dx(-1), me.dx(1)
        arrived(da_all.at[low], x_send.at[0], x_recv.at[0], mate)
        part = da_all.at[low, :, pl.ds(0, half)]
        x_sends(part, part, x_recv.at[2], up_x)
        arrived(da_all.at[high], x_send.at[0], x_recv.at[1], mate)
        part = da_all.at[high, :, pl.ds(half, half)]
        x_sends(part, part, x_recv.at[3], down_x)

    def x_end():
        far = me.dx(2)
        arrived(da_all.at[far, :, pl.ds(0, half)], x_send.at[0], x_recv.at[2], mate)
        arrived(da_all.at[far, :, pl.ds(half, half)], x_send.at[0], x_recv.at[3], mate)
        w_copy.wait()

    def product(at):
        width = 256
        rows = da_all[...].reshape(ROWS, da_ref.shape[1])
        g_ref[:, at * width:(at + 1) * width] = lax.dot_general(
            rows, w_all[at * width:(at + 1) * width, :], (((1,), (1,)), ((), ())),
            preferred_element_type=F32,
        ).astype(BF16)

    def to_mate(src, dst):
        pltpu.make_async_remote_copy(
            src_ref=src, dst_ref=dst, send_sem=mate_send, recv_sem=mate_recv,
            device_id=mate, device_id_type=MESH,
        ).start()

    def finish(core, sends):
        theirs = kv_ref.at[:, :, :, 1 - core]
        ours = kv_ref.at[:, :, :, core]
        arrived(theirs, mate_send, mate_recv, mate)
        pltpu.make_async_remote_copy(
            src_ref=ours, dst_ref=ours, send_sem=mate_send, recv_sem=mate_recv,
            device_id=mate, device_id_type=MESH,
        ).wait_send()
        sends.wait()
        x_sends.wait()

    up_z, down_z = me.device(z=me.dz(1)), me.device(z=me.dz(-1))
    up_y, down_y = me.device(y=me.dy(1)), me.device(y=me.dy(-1))

    def fetch(core, sends, step_y, step_z, devices, wait=True):
        py, pz = me.dy(step_y), me.dz(step_z)
        dst = piece(kv_ref, py, pz, core)
        sem = recv_sem.at[py * 8 + pz[0]]
        src = dst if wait else own
        if wait:
            arrived(dst, mate_send, sem, mate)
        for device in devices:
            sends(src, dst, sem, device)
        to_mate(src, dst)

    @pl.when(me.core == 0)
    def _():
        sends = Sends(send_sem)
        fetch(0, sends, 0, 0, [up_y, down_y, me.device(y=me.dy(2)), up_z, down_z], wait=False)
        x_start()
        for i in (1, -1, 2):
            fetch(0, sends, i, 0, [up_z, down_z])
        for s in (1, 2, 3):
            for i in (0, 1, -1, 2):
                fetch(0, sends, i, -s, [up_z] if s < 3 or i in (0, 1) else [])
                fetch(0, sends, i, s, [down_z] if s < 3 or i in (-1, 2) else [])
            if s == 2:
                x_middle()
        x_end()
        for at, i in enumerate((0, -1, 1, 2)):
            product(at)
            fetch(0, sends, i, 4, [])
        finish(0, sends)

    @pl.when(me.core == 1)
    def _():
        sends = Sends(send_sem)
        fetch(1, sends, 0, 0, [up_z, down_z, up_y, down_y], wait=False)
        x_start()

        def across(s):
            fetch(1, sends, -1, s, [up_y] if s <= 0 else [])
            fetch(1, sends, 1, s, [down_y] if s > 0 else [])

        for s in (1, 2, 3):
            fetch(1, sends, 0, -s, [up_z, up_y, down_y])
            fetch(1, sends, 0, s, ([down_z] if s < 3 else []) + [up_y, down_y])
            for r in ((0,) if s == 1 else (1 - s, s - 1)):
                across(r)
        fetch(1, sends, 0, 4, [up_y, down_y])
        x_middle()
        across(-3)
        across(3)
        across(4)
        x_end()
        for at in range(4):
            product(at)
            for s in ((0, -1), (1, -2), (2, -3), (3, 4))[at]:
                fetch(1, sends, 2, s, [])
        finish(1, sends)

    own_copy.wait()


def gather(k, v, da, w):
    return pl.pallas_call(
        gather_kernel,
        out_shape=(
            jax.ShapeDtypeStruct(PIECES, BF16),
            jax.ShapeDtypeStruct((ROWS, w.shape[0]), BF16),
        ),
        in_specs=[VMEM, VMEM, VMEM, ANY],
        out_specs=(ANY, VMEM),
        scratch_shapes=[
            pltpu.VMEM((ROWS, 2 * D), BF16),
            pltpu.VMEM((4,) + da.shape, BF16),
            pltpu.VMEM(w.shape, BF16),
            pltpu.SemaphoreType.DMA((2,)),
            pltpu.SemaphoreType.DMA((48,)),
            pltpu.SemaphoreType.DMA((32,)),
            pltpu.SemaphoreType.DMA,
            pltpu.SemaphoreType.DMA,
            pltpu.SemaphoreType.DMA((4,)),
            pltpu.SemaphoreType.DMA((4,)),
        ],
        compiler_params=pltpu.CompilerParams(
            collective_id=0, has_side_effects=True, vmem_limit_bytes=LIMIT
        ),
        name="gather",
    )(k, v, da, w)


def attention_kernel(
    seq_ref, order_ref, seg_ref, q_ref, g_ref, kv_ref, o_ref, dq_ref, dkv_ref,
    stored, qs, gs, q_t, g_t, weights, maxima, acc,
):
    seq = seq_ref[0]
    dkv_ref[...] = jnp.zeros_like(dkv_ref)
    for r in range(SPANS):
        stored[order_ref[r]] = r
    seg = seg_ref[...]
    starts = [jnp.sum((seg < d).astype(jnp.int32)) for d in range(1, 8)]
    key_iota = lax.broadcasted_iota(jnp.int32, (TILE, QROWS), 0)
    lane = lax.broadcasted_iota(jnp.int32, (1, QROWS), 1)

    def begin(position):
        first = jnp.zeros_like(position)
        for start in starts:
            first = jnp.maximum(first, jnp.where(start <= position, start, 0))
        return first

    def one_span(half, _):
        row = pl.multiple_of(half * SPAN, SPAN)
        span = order_ref[seq * 2 + half]
        position = span * SPAN + lax.rem(lane, SPAN)
        first = begin(position)
        span_0 = lax.div(begin(span * SPAN), SPAN)
        tiles = lax.div(span - span_0 + TILE_SPANS, TILE_SPANS)
        for h in range(HEADS):
            qs[h * SPAN:(h + 1) * SPAN, :] = q_ref[pl.ds(row, SPAN), h * D:(h + 1) * D]
            gs[h * SPAN:(h + 1) * SPAN, :] = g_ref[pl.ds(row, SPAN), h * D:(h + 1) * D]
        q_t[...] = qs[...].T
        g_t[...] = gs[...].T

        def rows_of(tile):
            return [
                pl.multiple_of(
                    stored[jnp.minimum(span_0 + tile * TILE_SPANS + b, SPANS - 1)] * SPAN, SPAN
                )
                for b in range(TILE_SPANS)
            ]

        def load(rows, column):
            return jnp.concatenate(
                [kv_ref[pl.ds(r, SPAN), column * D:(column + 1) * D] for r in rows], axis=0
            )

        acc[...] = jnp.zeros_like(acc)

        def forward(tile, carried):
            top, total = carried
            rows = rows_of(tile)
            scores = jnp.dot(load(rows, 0), q_t[...], preferred_element_type=F32)
            place = key_iota + (span_0 + tile * TILE_SPANS) * SPAN
            scores = jnp.where((place >= first) & (place <= position), scores, -1e30)
            new = jnp.maximum(top, jnp.max(scores, axis=0, keepdims=True))
            shrink = jnp.exp2((top - new) * EXP2_SCALE)
            exponent = jnp.exp2((scores - new) * EXP2_SCALE)
            total = total * shrink + jnp.sum(exponent, axis=0, keepdims=True)
            rounded = exponent.astype(BF16)
            weights[tile] = rounded
            maxima[tile] = new
            acc[...] = acc[...] * shrink + lax.dot_general(
                load(rows, 1), rounded, (((0,), (0,)), ((), ())), preferred_element_type=F32
            )
            return new, total

        top, total = lax.fori_loop(
            0, tiles, forward,
            (jnp.full((1, QROWS), -1e30, F32), jnp.zeros((1, QROWS), F32)),
        )
        inverse = 1.0 / total
        attended_t = (acc[...] * inverse).astype(BF16)
        delta = jnp.sum(
            attended_t.astype(F32) * g_t[...].astype(F32), axis=0, keepdims=True
        )
        attended = attended_t.T
        for h in range(HEADS):
            o_ref[pl.ds(row, SPAN), h * D:(h + 1) * D] = attended[h * SPAN:(h + 1) * SPAN, :]
        acc[...] = jnp.zeros_like(acc)

        def backward(tile, _):
            rows = rows_of(tile)
            factor = jnp.exp2((maxima[tile] - top) * EXP2_SCALE) * inverse
            d_prob = jnp.dot(load(rows, 1), g_t[...], preferred_element_type=F32)
            normed = weights[tile].astype(F32) * factor
            d_score = (normed * (d_prob - delta)).astype(BF16)
            acc[...] += lax.dot_general(
                load(rows, 0), d_score, (((0,), (0,)), ((), ())), preferred_element_type=F32
            )
            dk = jnp.dot(d_score, qs[...], preferred_element_type=F32)
            dv = jnp.dot(normed.astype(BF16), gs[...], preferred_element_type=F32)
            for b, r in enumerate(rows):
                for column, terms in enumerate((dk, dv)):
                    at = (pl.ds(r, SPAN), slice(column * D, (column + 1) * D))
                    dkv_ref[at] = (
                        dkv_ref[at].astype(F32) + terms[b * SPAN:(b + 1) * SPAN, :]
                    ).astype(BF16)
            return 0

        lax.fori_loop(0, tiles, backward, 0)
        dq = (acc[...] * SCALE).astype(BF16).T
        for h in range(HEADS):
            dq_ref[pl.ds(row, SPAN), h * D:(h + 1) * D] = dq[h * SPAN:(h + 1) * SPAN, :]
        return 0

    lax.fori_loop(0, 2, one_span, 0)


def attention(seq, order, seg, q, g, kv):
    return pl.pallas_call(
        attention_kernel,
        out_shape=(
            jax.ShapeDtypeStruct(q.shape, BF16),
            jax.ShapeDtypeStruct(q.shape, BF16),
            jax.ShapeDtypeStruct(kv.shape, BF16),
        ),
        in_specs=[SMEM, SMEM, VMEM, VMEM, VMEM, VMEM],
        out_specs=(VMEM, VMEM, VMEM),
        scratch_shapes=[
            pltpu.SMEM((SPANS,), jnp.int32),
            pltpu.VMEM((QROWS, D), BF16),
            pltpu.VMEM((QROWS, D), BF16),
            pltpu.VMEM((D, QROWS), BF16),
            pltpu.VMEM((D, QROWS), BF16),
            pltpu.VMEM((MAX_TILES, TILE, QROWS), BF16),
            pltpu.VMEM((MAX_TILES, 1, QROWS), F32),
            pltpu.VMEM((D, QROWS), F32),
        ],
        compiler_params=pltpu.CompilerParams(vmem_limit_bytes=LIMIT),
        name="attention",
    )(seq, order, seg, q, g, kv)


FAR_FIRST = (4, 3, -3, 2, -2, 1, -1, 0)
UPWARD = (4, -3, 2, -1)


def scatter_kernel(
    part_ref, dk_ref, dv_ref, mine, theirs, landed, load_sem, send_sem, recv_sem, mate_send, mate_recv
):
    me = Place()
    y, z = me.y, me.z
    mate = me.device(core=1 - me.core)

    @pl.when(me.core == 0)
    def _():
        for s in FAR_FIRST:
            pz = me.dz(s)
            pltpu.make_async_copy(
                part_ref.at[:, pz[1], pz[2], 0],
                mine.at[:, pz[1], pz[2]], load_sem.at[pz[0]],
            ).start()

    @pl.when(me.core == 1)
    def _():
        for s in (2, 1, -1, 0):
            py = me.dy(s)
            pltpu.make_async_copy(
                part_ref.at[py, :, :, 1], mine.at[py], load_sem.at[py]
            ).start()

    me.greet(
        [mate]
        + [me.device(y=me.dy(s)) for s in (1, -1, 2)]
        + [me.device(z=me.dz(s)) for s in (1, -1)]
    )
    up_z, down_z = me.device(z=me.dz(1)), me.device(z=me.dz(-1))
    up_y, down_y = me.device(y=me.dy(1)), me.device(y=me.dy(-1))

    def write(total):
        dk_ref[...] = (total[:, :D] * SCALE).astype(BF16)
        dv_ref[...] = total[:, D:].astype(BF16)

    def terms(py, pz, slots):
        at = (py, pz[1], pz[2])
        total = mine[at].astype(F32) + theirs[at].astype(F32)
        for slot in slots:
            arrived(landed.at[slot], mate_send.at[0], recv_sem.at[slot], mate)
            total = total + landed[slot].astype(F32)
        return at, total

    def pass_on(sends, py, pz, slots, slot, device):
        at, total = terms(py, pz, slots)
        mine[at] = total.astype(BF16)
        sends(mine.at[at], landed.at[slot], recv_sem.at[slot], device)

    @pl.when(me.core == 0)
    def _():
        sends = Sends(send_sem)
        mate_sends = Sends(mate_send)
        for s in (2, 1, -1, 0):
            py = me.dy(s)
            mate_sends(part_ref.at[py, :, :, 1], theirs.at[py], mate_recv.at[py], mate)

        def ready(s):
            pz = me.dz(s)
            at = (slice(None), pz[1], pz[2])
            pltpu.make_async_copy(part_ref.at[at + (0,)], mine.at[at], load_sem.at[pz[0]]).wait()
            arrived(theirs.at[at], mate_send.at[0], mate_recv.at[pz[0]], mate)

        order = (0, 1, -1, 2)
        up_slot = lambda s, i: (s - 1) * 4 + order.index(i)
        down_slot = lambda s, i: 16 + (s - 1) * 4 + order.index(i)
        ready(4)
        for i in (0, -1, 1, 2):
            if i in (0, 1):
                pass_on(sends, me.dy(i), me.dz(4), (), up_slot(4, i), up_z)
            else:
                pass_on(sends, me.dy(i), me.dz(4), (), down_slot(4, i), down_z)
        for s in (3, 2, 1):
            ready(s)
            ready(-s)
            for i in order:
                got = (up_slot(s + 1, i),) if s < 3 or i in (0, 1) else ()
                pass_on(sends, me.dy(i), me.dz(s), got, up_slot(s, i), up_z)
                got = (down_slot(s + 1, i),) if s < 3 or i in (-1, 2) else ()
                pass_on(sends, me.dy(i), me.dz(-s), got, down_slot(s, i), down_z)
        ready(0)
        for i in (1, -1, 2):
            pass_on(
                sends, me.dy(i), z, (up_slot(1, i), down_slot(1, i)),
                32 + order.index(i), me.device(y=me.dy(i)),
            )
        _, total = terms(y, z, (up_slot(1, 0), down_slot(1, 0), 33, 34, 35))
        write(total)
        mate_sends.wait()
        sends.wait()

    @pl.when(me.core == 1)
    def _():
        sends = Sends(send_sem)
        mate_sends = Sends(mate_send)
        for s in FAR_FIRST:
            pz = me.dz(s)
            at = (slice(None), pz[1], pz[2])
            mate_sends(part_ref.at[at + (0,)], theirs.at[at], mate_recv.at[pz[0]], mate)

        def ready(s):
            py = me.dy(s)
            pltpu.make_async_copy(part_ref.at[py, :, :, 1], mine.at[py], load_sem.at[py]).wait()
            arrived(theirs.at[py], mate_send.at[0], mate_recv.at[py], mate)

        index = FAR_FIRST.index
        ready(2)
        for s in FAR_FIRST:
            if s in UPWARD:
                pass_on(sends, me.dy(2), me.dz(s), (), index(s), up_y)
            else:
                pass_on(sends, me.dy(2), me.dz(s), (), index(s), down_y)
        ready(1)
        ready(-1)
        for s in FAR_FIRST:
            got = (index(s),)
            pass_on(sends, me.dy(1), me.dz(s), got if s in UPWARD else (), 8 + index(s), up_y)
            pass_on(sends, me.dy(-1), me.dz(s), () if s in UPWARD else got, 16 + index(s), down_y)
        ready(0)
        for s in FAR_FIRST:
            got = (8 + index(s), 16 + index(s))
            if s > 0:
                got += (24 + s + 1,) if s < 4 else ()
                pass_on(sends, y, me.dz(s), got, 24 + s, up_z)
            elif s < 0:
                got += (32 - s + 1,) if s > -3 else ()
                pass_on(sends, y, me.dz(s), got, 32 - s, down_z)
            else:
                _, total = terms(y, z, got + (25, 33))
                write(total)
        mate_sends.wait()
        sends.wait()


def scatter(part):
    return pl.pallas_call(
        scatter_kernel,
        out_shape=(
            jax.ShapeDtypeStruct((ROWS, D), BF16),
            jax.ShapeDtypeStruct((ROWS, D), BF16),
        ),
        in_specs=[ANY],
        out_specs=(VMEM, VMEM),
        scratch_shapes=[
            pltpu.VMEM((4, 2, 4, ROWS, 2 * D), BF16),
            pltpu.VMEM((4, 2, 4, ROWS, 2 * D), BF16),
            pltpu.VMEM((36, ROWS, 2 * D), BF16),
            pltpu.SemaphoreType.DMA((8,)),
            pltpu.SemaphoreType.DMA((40,)),
            pltpu.SemaphoreType.DMA((36,)),
            pltpu.SemaphoreType.DMA((8,)),
            pltpu.SemaphoreType.DMA((8,)),
        ],
        compiler_params=pltpu.CompilerParams(
            collective_id=1, has_side_effects=True, vmem_limit_bytes=LIMIT
        ),
        name="scatter",
    )(part)


def shards(
    query_matrix, key_matrix, value_matrix, segment_ids, block_order, out_weight, d_attended
):
    seq = lax.axis_index(("inner", "outer")).astype(jnp.int32).reshape(1)
    pieces, g = gather(key_matrix, value_matrix, d_attended, out_weight)
    attended, d_queries, terms = attention(
        seq, block_order, segment_ids.reshape(64, 128), query_matrix, g,
        pieces.reshape(TOKENS, 2 * D),
    )
    key_gradient, value_gradient = scatter(terms.reshape(PIECES))
    return (attended, d_queries, key_gradient, value_gradient)


def solution(mesh):
    return jax.shard_map(
        shards,
        mesh=mesh,
        in_specs=(
            P(("inner", "outer"), "tensor"),
            P(("inner", "outer"), "tensor"),
            P(("inner", "outer"), "tensor"),
            P(),
            P(),
            P("tensor", None),
            P(("inner", "outer", "tensor"), None),
        ),
        out_specs=(
            P(("inner", "outer"), "tensor"),
            P(("inner", "outer"), "tensor"),
            P(("inner", "outer"), "tensor"),
            P(("inner", "outer"), "tensor"),
        ),
        check_vma=False,
    )
```

time: 589 us -> 93.7 us (0.16); the launches traced: 579 us -> 92.5 us
  waiting for transfers between devices: 359 us -> 0 us
  local copies, waits for them, and re-layouts: 104 us -> 2.75 us
  Pallas kernels: 0 us -> 89.1 us
  matrix products: 76.4 us -> 0 us
  other arithmetic: 25.2 us -> 0 us
  between operations: 13.9 us -> 0.66 us
    reduce_scatter x1 -> x0, waiting for transfers between devices: 266 us -> none  [shards(): lax.psum_scatter(all_terms, ('inner', 'outer'), scatter_dimension=0, tile...]
    all_gather x2 -> x0, waiting for transfers between devices: 92.2 us -> none  [the longest x1 92.2 us: shards(): gathered = lax.all_gather(paired, ('inner', 'outer'), axis=0, tiled=True)]
    pallas_call x0 -> x3, Pallas kernels: none -> 89.1 us  [the longest x1 44.2 us: scatter(): pl.pallas_call(scatter_kernel, out_shape=(jax.ShapeDtypeStruct((ROWS, D),...]
    dot_general x49 -> x0, matrix products: 76.4 us -> none  [the longest x8 25 us: head_pass(): jnp.einsum('kad,qad->kaq', heads_of_keys, query_head, preferred_element_t...]
    while x82 -> x0, local copies, waits for them, and re-layouts: 51.6 us -> none
    gather x1 -> x0, local copies, waits for them, and re-layouts: 45.5 us -> none  [token_places(): return (places, jnp.take(segment_ids, places))]
    reduce_sum x9 -> x0, other arithmetic: 15 us -> none  [the longest x8 11.7 us: head_pass(): row_sum = jnp.sum(exponent, axis=0)]
    concatenate x2 -> x0, other arithmetic: 8.65 us -> none  [the longest x1 7.24 us: shards(): jnp.concatenate([term_sums[0].reshape(total_rows, kv_width), term_sums[1]...]
  transfers between devices with their start and end apart: 3 -> 0, of which waited for: 2 -> 0; matrix products, arithmetic and copies ran while one was open for 10% -> 0% of each run, Pallas kernels for 0% -> 0%
where the time goes in v1:
time: 93.7 us; the launch traced here: 92.5 us
  Pallas kernels  89.1 us (95%)
  local copies, waits for them, and re-layouts  2.75 us (3%)
    pallas_call x1, Pallas kernels, scatter(): pl.pallas_call(scatter_kernel, out_shape=(jax.ShapeDtypeStruct((ROWS, D),...  44.2 us
    pallas_call x1, Pallas kernels, gather(): pl.pallas_call(gather_kernel, out_shape=(jax.ShapeDtypeStruct(PIECES, BF1...  34.9 us
    pallas_call x1, Pallas kernels, attention(): pl.pallas_call(attention_kernel, out_shape=(jax.ShapeDtypeStruct(q.shape,...  10 us
    unnamed x2, local copies, waits for them, and re-layouts  2.75 us

profile of v1, /device:TPU:32, one launch (start us, length us, event | category | flops | bytes accessed | tf_op | source)
XLA Modules:
  0.0 92.5 jit_solution(8961259815991225060)
XLA Ops:
  0.6 34.9 %gather.1 = (bf16[4,2,4,2,128,256]{5,4,3,2,1,0:T(8,128)(2,1)}, bf16[128,1024]{1,0:T(8,128)(2,1)}) custom-call(bf16[128,128]{1,0:T(8,128)(2,1)} %k_ref.1, bf16[128,128]{1,0:T(8,128)(2,1)} %v_ref.1, bf16[32,4096]{1,0:T(8,128)(2,1)} %da_ref.1, bf16[1024,4096]{1,0:T(8,128)(2,1)} %w_ref.1), custom_call_target="tpu_custom_call" | custom-call | tf_op jit(solution)/shard_map/gather/pallas_call | solution.py:230
  35.5 10.0 %attention.1 = (bf16[128,1024]{1,0:T(8,128)(2,1)}, bf16[128,1024]{1,0:T(8,128)(2,1)}, bf16[8192,256]{1,0:T(8,128)(2,1)}) custom-call(s32[1]{0:T(128)} %bitcast.seq_ref, s32[128]{0:T(128)} %order_ref.1, s32[64,128]{1,0:T(8,128)} %bitcast.6, bf16[128,1024]{1,0:T(8,128)(2,1)} %q_ref.1, bf16[128,1024]{1,0:T(8,128)(2,1)} %get-tuple-element.11.g_ref, ...), custom_call_target="tpu_custom_call" | custom-call | tf_op jit(solution)/shard_map/attention/pallas_call | solution.py:365
  45.5 44.2 %scatter.1 = (bf16[128,128]{1,0:T(8,128)(2,1)}, bf16[128,128]{1,0:T(8,128)(2,1)}) custom-call(bf16[4,2,4,2,128,256]{5,4,3,2,1,0:T(8,128)(2,1)} %bitcast.4), custom_call_target="tpu_custom_call" | custom-call | tf_op jit(solution)/shard_map/scatter/pallas_call | solution.py:528
  89.8 1.4 %copy.13 = bf16[128,128]{1,0:T(8,128)(2,1)} copy(bf16[128,128]{1,0:T(8,128)(2,1)} %get-tuple-element.24) | data formatting | bytes 65536
  91.1 1.4 %copy.14 = bf16[128,128]{1,0:T(8,128)(2,1)} copy(bf16[128,128]{1,0:T(8,128)(2,1)} %get-tuple-element.25) | data formatting | bytes 65536

commit v2 on v1

--- a/solution.py
+++ b/solution.py
@@ -15,9 +15,12 @@
 SPANS = 128
 TOKENS = 8192
 QROWS = SPAN * HEADS
-TILE_SPANS = 8
-TILE = TILE_SPANS * SPAN
-MAX_TILES = 65 // TILE_SPANS + 1
+UNIT = 8
+SIZES = (4, 2, 1)
+CHUNK = 128
+PER_SUM = 8
+LOADS = 8
+MOST_KEYS = (65 + UNIT - 1) // UNIT * UNIT * SPAN
 SCALE = 1.0 / math.sqrt(D)
 EXP2_SCALE = SCALE * math.log2(math.e)
 F32 = jnp.float32
@@ -112,7 +115,7 @@
     me.greet(
         [mate]
         + [me.device(y=me.dy(s)) for s in (1, -1, 2)]
-        + [me.device(z=me.dz(s)) for s in (1, -1)]
+        + [me.device(z=me.dz(s)) for s in (1, -1, 2, -2)]
         + [me.device(x=me.dx(s)) for s in (1, -1)]
     )
     up_x, down_x = me.device(x=me.dx(1)), me.device(x=me.dx(-1))
@@ -164,6 +167,7 @@
         x_sends.wait()
 
     up_z, down_z = me.device(z=me.dz(1)), me.device(z=me.dz(-1))
+    up_2z, down_2z = me.device(z=me.dz(2)), me.device(z=me.dz(-2))
     up_y, down_y = me.device(y=me.dy(1)), me.device(y=me.dy(-1))
 
     def fetch(core, sends, step_y, step_z, devices, wait=True):
@@ -184,33 +188,43 @@
         x_start()
         for i in (1, -1, 2):
             fetch(0, sends, i, 0, [up_z, down_z])
-        for s in (1, 2, 3):
-            for i in (0, 1, -1, 2):
-                fetch(0, sends, i, -s, [up_z] if s < 3 or i in (0, 1) else [])
-                fetch(0, sends, i, s, [down_z] if s < 3 or i in (-1, 2) else [])
-            if s == 2:
-                x_middle()
+        for i in (0, 1, -1, 2):
+            fetch(0, sends, i, -1, [up_z])
+            fetch(0, sends, i, 1, [down_z])
+        x_middle()
+        for i in (0, 1, -1, 2):
+            fetch(0, sends, i, -2, [up_2z, up_z] if i in (0, 1) else [up_z])
+            fetch(0, sends, i, 2, [down_2z, down_z] if i in (-1, 2) else [down_z])
         x_end()
-        for at, i in enumerate((0, -1, 1, 2)):
+        for at, i in enumerate((0, 1, -1, 2)):
             product(at)
+            fetch(0, sends, i, -3, [])
+            fetch(0, sends, i, 3, [])
+        for i in (0, -1, 1, 2):
             fetch(0, sends, i, 4, [])
         finish(0, sends)
 
     @pl.when(me.core == 1)
     def _():
         sends = Sends(send_sem)
-        fetch(1, sends, 0, 0, [up_z, down_z, up_y, down_y], wait=False)
+        fetch(1, sends, 0, 0, [up_z, down_z, up_2z, down_2z, up_y, down_y], wait=False)
         x_start()
 
         def across(s):
             fetch(1, sends, -1, s, [up_y] if s <= 0 else [])
             fetch(1, sends, 1, s, [down_y] if s > 0 else [])
 
-        for s in (1, 2, 3):
-            fetch(1, sends, 0, -s, [up_z, up_y, down_y])
-            fetch(1, sends, 0, s, ([down_z] if s < 3 else []) + [up_y, down_y])
-            for r in ((0,) if s == 1 else (1 - s, s - 1)):
-                across(r)
+        fetch(1, sends, 0, -1, [up_y, down_y])
+        fetch(1, sends, 0, 1, [up_y, down_y])
+        across(0)
+        fetch(1, sends, 0, -2, [up_2z, up_z, up_y, down_y])
+        fetch(1, sends, 0, 2, [down_z, up_y, down_y])
+        across(-1)
+        across(1)
+        fetch(1, sends, 0, -3, [up_y, down_y])
+        fetch(1, sends, 0, 3, [up_y, down_y])
+        across(-2)
+        across(2)
         fetch(1, sends, 0, 4, [up_y, down_y])
         x_middle()
         across(-3)
@@ -256,15 +270,24 @@
 
 def attention_kernel(
     seq_ref, order_ref, seg_ref, q_ref, g_ref, kv_ref, o_ref, dq_ref, dkv_ref,
-    stored, qs, gs, q_t, g_t, weights, maxima, acc,
+    kv, load_sem, stored, qs, gs, q_t, g_t, scores, weights, d_scores, acc,
 ):
+    chunk = TOKENS // LOADS
+    loads = [
+        pltpu.make_async_copy(
+            kv_ref.at[pl.ds(c * chunk, chunk)], kv.at[pl.ds(c * chunk, chunk)], load_sem.at[c]
+        )
+        for c in range(LOADS)
+    ]
+    for copy in loads:
+        copy.start()
     seq = seq_ref[0]
-    dkv_ref[...] = jnp.zeros_like(dkv_ref)
     for r in range(SPANS):
         stored[order_ref[r]] = r
     seg = seg_ref[...]
     starts = [jnp.sum((seg < d).astype(jnp.int32)) for d in range(1, 8)]
-    key_iota = lax.broadcasted_iota(jnp.int32, (TILE, QROWS), 0)
+    dkv_ref[...] = jnp.zeros_like(dkv_ref)
+    key_iota = lax.broadcasted_iota(jnp.int32, (CHUNK, QROWS), 0)
     lane = lax.broadcasted_iota(jnp.int32, (1, QROWS), 1)
 
     def begin(position):
@@ -272,6 +295,9 @@
         for start in starts:
             first = jnp.maximum(first, jnp.where(start <= position, start, 0))
         return first
+
+    for copy in loads:
+        copy.wait()
 
     def one_span(half, _):
         row = pl.multiple_of(half * SPAN, SPAN)
@@ -279,80 +305,115 @@
         position = span * SPAN + lax.rem(lane, SPAN)
         first = begin(position)
         span_0 = lax.div(begin(span * SPAN), SPAN)
-        tiles = lax.div(span - span_0 + TILE_SPANS, TILE_SPANS)
+        units = lax.div(span - span_0 + UNIT, UNIT)
         for h in range(HEADS):
             qs[h * SPAN:(h + 1) * SPAN, :] = q_ref[pl.ds(row, SPAN), h * D:(h + 1) * D]
             gs[h * SPAN:(h + 1) * SPAN, :] = g_ref[pl.ds(row, SPAN), h * D:(h + 1) * D]
         q_t[...] = qs[...].T
         g_t[...] = gs[...].T
 
-        def rows_of(tile):
+        def tiles(step, carried):
+            done = 0
+            for size in SIZES:
+                count = lax.div(units - done, size)
+                carried = lax.fori_loop(
+                    0, count,
+                    lambda i, c, size=size, done=done: step(
+                        (done + i * size) * UNIT, size * UNIT, c
+                    ),
+                    carried,
+                )
+                done = done + count * size
+            return carried
+
+        def rows_of(at, count):
             return [
-                pl.multiple_of(
-                    stored[jnp.minimum(span_0 + tile * TILE_SPANS + b, SPANS - 1)] * SPAN, SPAN
-                )
-                for b in range(TILE_SPANS)
+                pl.multiple_of(stored[jnp.minimum(span_0 + at + b, SPANS - 1)] * SPAN, SPAN)
+                for b in range(count)
             ]
 
         def load(rows, column):
             return jnp.concatenate(
-                [kv_ref[pl.ds(r, SPAN), column * D:(column + 1) * D] for r in rows], axis=0
+                [kv[pl.ds(r, SPAN), column * D:(column + 1) * D] for r in rows], axis=0
             )
 
+        def keys(at, offset, size):
+            return pl.ds(pl.multiple_of(at * SPAN, SPAN) + offset, size)
+
+        per = CHUNK // SPAN
+
+        def score(at, count, best):
+            rows = rows_of(at, count)
+            base = (span_0 + at) * SPAN
+            low, high = first - base, position - base
+            for c in range(count // per):
+                raw = jnp.dot(
+                    load(rows[c * per:(c + 1) * per], 0), q_t[...], preferred_element_type=F32
+                )
+                place = key_iota + c * CHUNK
+                raw = jnp.where((place >= low) & (place <= high), raw, -1e30)
+                scores[keys(at, c * CHUNK, CHUNK), :] = raw
+                best = jnp.maximum(best, jnp.max(raw.reshape(CHUNK // 8, 8, QROWS), axis=0))
+            return best
+
+        best = tiles(score, jnp.full((8, QROWS), -1e30, F32))
+        top = jnp.max(best, axis=0, keepdims=True) * EXP2_SCALE
         acc[...] = jnp.zeros_like(acc)
 
-        def forward(tile, carried):
-            top, total = carried
-            rows = rows_of(tile)
-            scores = jnp.dot(load(rows, 0), q_t[...], preferred_element_type=F32)
-            place = key_iota + (span_0 + tile * TILE_SPANS) * SPAN
-            scores = jnp.where((place >= first) & (place <= position), scores, -1e30)
-            new = jnp.maximum(top, jnp.max(scores, axis=0, keepdims=True))
-            shrink = jnp.exp2((top - new) * EXP2_SCALE)
-            exponent = jnp.exp2((scores - new) * EXP2_SCALE)
-            total = total * shrink + jnp.sum(exponent, axis=0, keepdims=True)
-            rounded = exponent.astype(BF16)
-            weights[tile] = rounded
-            maxima[tile] = new
-            acc[...] = acc[...] * shrink + lax.dot_general(
-                load(rows, 1), rounded, (((0,), (0,)), ((), ())), preferred_element_type=F32
+        def forward(at, count, total):
+            for c in range(count // per):
+                part = keys(at, c * CHUNK, CHUNK)
+                exponent = jnp.exp2(scores[part, :] * EXP2_SCALE - top)
+                weights[part, :] = exponent.astype(BF16)
+                total = total + jnp.sum(exponent.reshape(CHUNK // 8, 8, QROWS), axis=0)
+            acc[...] += lax.dot_general(
+                load(rows_of(at, count), 1), weights[keys(at, 0, count * SPAN), :],
+                (((0,), (0,)), ((), ())), preferred_element_type=F32,
             )
-            return new, total
-
-        top, total = lax.fori_loop(
-            0, tiles, forward,
-            (jnp.full((1, QROWS), -1e30, F32), jnp.zeros((1, QROWS), F32)),
-        )
-        inverse = 1.0 / total
+            return total
+
+        total = tiles(forward, jnp.zeros((8, QROWS), F32))
+        inverse = 1.0 / jnp.sum(total, axis=0, keepdims=True)
         attended_t = (acc[...] * inverse).astype(BF16)
-        delta = jnp.sum(
-            attended_t.astype(F32) * g_t[...].astype(F32), axis=0, keepdims=True
-        )
         attended = attended_t.T
         for h in range(HEADS):
             o_ref[pl.ds(row, SPAN), h * D:(h + 1) * D] = attended[h * SPAN:(h + 1) * SPAN, :]
+        shrunk = (g_t[...].astype(F32) * inverse).astype(BF16)
+        g_t[...] = shrunk
+        gs[...] = shrunk.T
+        delta = jnp.sum(
+            attended_t.astype(F32) * shrunk.astype(F32), axis=0, keepdims=True
+        )
         acc[...] = jnp.zeros_like(acc)
 
-        def backward(tile, _):
-            rows = rows_of(tile)
-            factor = jnp.exp2((maxima[tile] - top) * EXP2_SCALE) * inverse
-            d_prob = jnp.dot(load(rows, 1), g_t[...], preferred_element_type=F32)
-            normed = weights[tile].astype(F32) * factor
-            d_score = (normed * (d_prob - delta)).astype(BF16)
+        def backward(at, count, carried):
+            rows = rows_of(at, count)
+            for c in range(count // per):
+                d_prob = jnp.dot(
+                    load(rows[c * per:(c + 1) * per], 1), g_t[...], preferred_element_type=F32
+                )
+                weight = weights[keys(at, c * CHUNK, CHUNK), :].astype(F32)
+                d_scores[c * CHUNK:(c + 1) * CHUNK, :] = (weight * (d_prob - delta)).astype(BF16)
             acc[...] += lax.dot_general(
-                load(rows, 0), d_score, (((0,), (0,)), ((), ())), preferred_element_type=F32
+                load(rows, 0), d_scores[:count * SPAN, :], (((0,), (0,)), ((), ())),
+                preferred_element_type=F32,
             )
-            dk = jnp.dot(d_score, qs[...], preferred_element_type=F32)
-            dv = jnp.dot(normed.astype(BF16), gs[...], preferred_element_type=F32)
-            for b, r in enumerate(rows):
-                for column, terms in enumerate((dk, dv)):
-                    at = (pl.ds(r, SPAN), slice(column * D, (column + 1) * D))
-                    dkv_ref[at] = (
-                        dkv_ref[at].astype(F32) + terms[b * SPAN:(b + 1) * SPAN, :]
-                    ).astype(BF16)
-            return 0
-
-        lax.fori_loop(0, tiles, backward, 0)
+            for c in range(count // PER_SUM):
+                part = slice(c * PER_SUM * SPAN, (c + 1) * PER_SUM * SPAN)
+                dk = jnp.dot(d_scores[part, :], qs[...], preferred_element_type=F32)
+                dv = jnp.dot(
+                    weights[keys(at, c * PER_SUM * SPAN, PER_SUM * SPAN), :], gs[...],
+                    preferred_element_type=F32,
+                )
+                for b, r in enumerate(rows[c * PER_SUM:(c + 1) * PER_SUM]):
+                    for column, terms in enumerate((dk, dv)):
+                        place = (pl.ds(r, SPAN), slice(column * D, (column + 1) * D))
+                        dkv_ref[place] = (
+                            dkv_ref[place].astype(F32) + terms[b * SPAN:(b + 1) * SPAN, :]
+                        ).astype(BF16)
+            return carried
+
+        tiles(backward, 0)
         dq = (acc[...] * SCALE).astype(BF16).T
         for h in range(HEADS):
             dq_ref[pl.ds(row, SPAN), h * D:(h + 1) * D] = dq[h * SPAN:(h + 1) * SPAN, :]
@@ -369,16 +430,19 @@
             jax.ShapeDtypeStruct(q.shape, BF16),
             jax.ShapeDtypeStruct(kv.shape, BF16),
         ),
-        in_specs=[SMEM, SMEM, VMEM, VMEM, VMEM, VMEM],
+        in_specs=[SMEM, SMEM, VMEM, VMEM, VMEM, ANY],
         out_specs=(VMEM, VMEM, VMEM),
         scratch_shapes=[
+            pltpu.VMEM(kv.shape, BF16),
+            pltpu.SemaphoreType.DMA((LOADS,)),
             pltpu.SMEM((SPANS,), jnp.int32),
             pltpu.VMEM((QROWS, D), BF16),
             pltpu.VMEM((QROWS, D), BF16),
             pltpu.VMEM((D, QROWS), BF16),
             pltpu.VMEM((D, QROWS), BF16),
-            pltpu.VMEM((MAX_TILES, TILE, QROWS), BF16),
-            pltpu.VMEM((MAX_TILES, 1, QROWS), F32),
+            pltpu.VMEM((MOST_KEYS, QROWS), F32),
+            pltpu.VMEM((MOST_KEYS, QROWS), BF16),
+            pltpu.VMEM((max(SIZES) * UNIT * SPAN, QROWS), BF16),
             pltpu.VMEM((D, QROWS), F32),
         ],
         compiler_params=pltpu.CompilerParams(vmem_limit_bytes=LIMIT),
@@ -391,43 +455,46 @@
 
 
 def scatter_kernel(
-    part_ref, dk_ref, dv_ref, mine, theirs, landed, load_sem, send_sem, recv_sem, mate_send, mate_recv
+    part_ref, sum_ref, mine, theirs, landed, load_sem, send_sem, recv_sem, mate_send, mate_recv
 ):
     me = Place()
     y, z = me.y, me.z
     mate = me.device(core=1 - me.core)
 
+    def of_z(s):
+        return (slice(None),) + me.dz(s)[1:]
+
+    def load_z(s):
+        return pltpu.make_async_copy(
+            part_ref.at[of_z(s) + (0,)], mine.at[of_z(s)], load_sem.at[me.dz(s)[0]]
+        )
+
+    def load_y(s):
+        py = me.dy(s)
+        return pltpu.make_async_copy(part_ref.at[py, :, :, 1], mine.at[py], load_sem.at[py])
+
     @pl.when(me.core == 0)
     def _():
         for s in FAR_FIRST:
-            pz = me.dz(s)
-            pltpu.make_async_copy(
-                part_ref.at[:, pz[1], pz[2], 0],
-                mine.at[:, pz[1], pz[2]], load_sem.at[pz[0]],
-            ).start()
+            load_z(s).start()
 
     @pl.when(me.core == 1)
     def _():
         for s in (2, 1, -1, 0):
-            py = me.dy(s)
-            pltpu.make_async_copy(
-                part_ref.at[py, :, :, 1], mine.at[py], load_sem.at[py]
-            ).start()
+            load_y(s).start()
 
     me.greet(
         [mate]
         + [me.device(y=me.dy(s)) for s in (1, -1, 2)]
-        + [me.device(z=me.dz(s)) for s in (1, -1)]
+        + [me.device(z=me.dz(s)) for s in (1, -1, 2, -2)]
     )
     up_z, down_z = me.device(z=me.dz(1)), me.device(z=me.dz(-1))
+    up_2z, down_2z = me.device(z=me.dz(2)), me.device(z=me.dz(-2))
     up_y, down_y = me.device(y=me.dy(1)), me.device(y=me.dy(-1))
-
-    def write(total):
-        dk_ref[...] = (total[:, :D] * SCALE).astype(BF16)
-        dv_ref[...] = total[:, D:].astype(BF16)
+    index = FAR_FIRST.index
 
     def terms(py, pz, slots):
-        at = (py, pz[1], pz[2])
+        at = (py,) + pz[1:]
         total = mine[at].astype(F32) + theirs[at].astype(F32)
         for slot in slots:
             arrived(landed.at[slot], mate_send.at[0], recv_sem.at[slot], mate)
@@ -443,15 +510,18 @@
     def _():
         sends = Sends(send_sem)
         mate_sends = Sends(mate_send)
-        for s in (2, 1, -1, 0):
+        for s in FAR_FIRST:
+            at = (me.dy(2),) + me.dz(s)[1:]
+            mate_sends(
+                part_ref.at[at + (1,)], theirs.at[at], mate_recv.at[4 + index(s)], mate
+            )
+        for s in (1, -1, 0):
             py = me.dy(s)
             mate_sends(part_ref.at[py, :, :, 1], theirs.at[py], mate_recv.at[py], mate)
 
         def ready(s):
-            pz = me.dz(s)
-            at = (slice(None), pz[1], pz[2])
-            pltpu.make_async_copy(part_ref.at[at + (0,)], mine.at[at], load_sem.at[pz[0]]).wait()
-            arrived(theirs.at[at], mate_send.at[0], mate_recv.at[pz[0]], mate)
+            load_z(s).wait()
+            arrived(theirs.at[of_z(s)], mate_send.at[0], mate_recv.at[me.dz(s)[0]], mate)
 
         order = (0, 1, -1, 2)
         up_slot = lambda s, i: (s - 1) * 4 + order.index(i)
@@ -459,16 +529,18 @@
         ready(4)
         for i in (0, -1, 1, 2):
             if i in (0, 1):
-                pass_on(sends, me.dy(i), me.dz(4), (), up_slot(4, i), up_z)
+                pass_on(sends, me.dy(i), me.dz(4), (), up_slot(4, i), up_2z)
             else:
-                pass_on(sends, me.dy(i), me.dz(4), (), down_slot(4, i), down_z)
+                pass_on(sends, me.dy(i), me.dz(4), (), down_slot(4, i), down_2z)
         for s in (3, 2, 1):
             ready(s)
             ready(-s)
             for i in order:
-                got = (up_slot(s + 1, i),) if s < 3 or i in (0, 1) else ()
+                got = (up_slot(s + 1, i),) if s < 3 else ()
+                got += (up_slot(4, i),) if s == 2 and i in (0, 1) else ()
                 pass_on(sends, me.dy(i), me.dz(s), got, up_slot(s, i), up_z)
-                got = (down_slot(s + 1, i),) if s < 3 or i in (-1, 2) else ()
+                got = (down_slot(s + 1, i),) if s < 3 else ()
+                got += (down_slot(4, i),) if s == 2 and i in (-1, 2) else ()
                 pass_on(sends, me.dy(i), me.dz(-s), got, down_slot(s, i), down_z)
         ready(0)
         for i in (1, -1, 2):
@@ -477,7 +549,7 @@
                 32 + order.index(i), me.device(y=me.dy(i)),
             )
         _, total = terms(y, z, (up_slot(1, 0), down_slot(1, 0), 33, 34, 35))
-        write(total)
+        sum_ref[...] = total
         mate_sends.wait()
         sends.wait()
 
@@ -486,18 +558,18 @@
         sends = Sends(send_sem)
         mate_sends = Sends(mate_send)
         for s in FAR_FIRST:
-            pz = me.dz(s)
-            at = (slice(None), pz[1], pz[2])
-            mate_sends(part_ref.at[at + (0,)], theirs.at[at], mate_recv.at[pz[0]], mate)
+            at = of_z(s)
+            mate_sends(part_ref.at[at + (0,)], theirs.at[at], mate_recv.at[me.dz(s)[0]], mate)
 
         def ready(s):
             py = me.dy(s)
-            pltpu.make_async_copy(part_ref.at[py, :, :, 1], mine.at[py], load_sem.at[py]).wait()
+            load_y(s).wait()
             arrived(theirs.at[py], mate_send.at[0], mate_recv.at[py], mate)
 
-        index = FAR_FIRST.index
-        ready(2)
+        load_y(2).wait()
         for s in FAR_FIRST:
+            at = (me.dy(2),) + me.dz(s)[1:]
+            arrived(theirs.at[at], mate_send.at[0], mate_recv.at[4 + index(s)], mate)
             if s in UPWARD:
                 pass_on(sends, me.dy(2), me.dz(s), (), index(s), up_y)
             else:
@@ -509,17 +581,17 @@
             pass_on(sends, me.dy(1), me.dz(s), got if s in UPWARD else (), 8 + index(s), up_y)
             pass_on(sends, me.dy(-1), me.dz(s), () if s in UPWARD else got, 16 + index(s), down_y)
         ready(0)
-        for s in FAR_FIRST:
-            got = (8 + index(s), 16 + index(s))
-            if s > 0:
-                got += (24 + s + 1,) if s < 4 else ()
-                pass_on(sends, y, me.dz(s), got, 24 + s, up_z)
-            elif s < 0:
-                got += (32 - s + 1,) if s > -3 else ()
-                pass_on(sends, y, me.dz(s), got, 32 - s, down_z)
-            else:
-                _, total = terms(y, z, got + (25, 33))
-                write(total)
+        routes = {
+            4: ((), up_2z), 3: ((), up_z), -3: ((), down_z), 2: ((3, 4), up_2z),
+            -2: ((-3,), down_2z), 1: ((), up_z), -1: ((), down_z),
+        }
+        for s in FAR_FIRST[:-1]:
+            extra, device = routes[s]
+            got = (8 + index(s), 16 + index(s)) + tuple(24 + index(e) for e in extra)
+            pass_on(sends, y, me.dz(s), got, 24 + index(s), device)
+        got = (15, 23) + tuple(24 + index(e) for e in (1, -1, 2, -2))
+        _, total = terms(y, z, got)
+        sum_ref[...] = total
         mate_sends.wait()
         sends.wait()
 
@@ -527,12 +599,9 @@
 def scatter(part):
     return pl.pallas_call(
         scatter_kernel,
-        out_shape=(
-            jax.ShapeDtypeStruct((ROWS, D), BF16),
-            jax.ShapeDtypeStruct((ROWS, D), BF16),
-        ),
+        out_shape=jax.ShapeDtypeStruct((ROWS, 2 * D), F32),
         in_specs=[ANY],
-        out_specs=(VMEM, VMEM),
+        out_specs=VMEM,
         scratch_shapes=[
             pltpu.VMEM((4, 2, 4, ROWS, 2 * D), BF16),
             pltpu.VMEM((4, 2, 4, ROWS, 2 * D), BF16),
@@ -540,8 +609,8 @@
             pltpu.SemaphoreType.DMA((8,)),
             pltpu.SemaphoreType.DMA((40,)),
             pltpu.SemaphoreType.DMA((36,)),
-            pltpu.SemaphoreType.DMA((8,)),
-            pltpu.SemaphoreType.DMA((8,)),
+            pltpu.SemaphoreType.DMA((12,)),
+            pltpu.SemaphoreType.DMA((12,)),
         ],
         compiler_params=pltpu.CompilerParams(
             collective_id=1, has_side_effects=True, vmem_limit_bytes=LIMIT
@@ -559,7 +628,9 @@
         seq, block_order, segment_ids.reshape(64, 128), query_matrix, g,
         pieces.reshape(TOKENS, 2 * D),
     )
-    key_gradient, value_gradient = scatter(terms.reshape(PIECES))
+    sums = scatter(terms.reshape(PIECES))
+    key_gradient = (sums[:, :D] * SCALE).astype(BF16)
+    value_gradient = sums[:, D:].astype(BF16)
     return (attended, d_queries, key_gradient, value_gradient)
 
 

time: 93.7 us -> 88.6 us (0.946)
  Pallas kernels: 89.1 us -> 84.8 us
  other arithmetic: 0 us -> 1.46 us
  local copies, waits for them, and re-layouts: 2.75 us -> 1.46 us
    pallas_call x1, Pallas kernels: 44.2 us -> 40.1 us  [scatter(): pl.pallas_call(scatter_kernel, out_shape=jax.ShapeDtypeStruct((ROWS, 2 *...]
    unnamed x2 -> x0, local copies, waits for them, and re-layouts: 2.75 us -> none
    convert_element_type x0 -> x1, other arithmetic: none -> 1.46 us  [shards(): key_gradient = (sums[:, :D] * SCALE).astype(BF16)]
    slice x0 -> x1, local copies, waits for them, and re-layouts: none -> 1.46 us  [shards(): value_gradient = sums[:, D:].astype(BF16)]
    pallas_call x1, Pallas kernels: 34.9 us -> 33.6 us  [gather(): pl.pallas_call(gather_kernel, out_shape=(jax.ShapeDtypeStruct(PIECES, BF1...]
    pallas_call x1, Pallas kernels: 10 us -> 11.1 us  [attention(): pl.pallas_call(attention_kernel, out_shape=(jax.ShapeDtypeStruct(q.shape,...]
where the time goes in v2:
time: 88.6 us; the launch traced here: 88.3 us
  Pallas kernels  84.8 us (96%)
  local copies, waits for them, and re-layouts  1.46 us (2%)
  other arithmetic  1.46 us (2%)
    pallas_call x1, Pallas kernels, scatter(): pl.pallas_call(scatter_kernel, out_shape=jax.ShapeDtypeStruct((ROWS, 2 *...  40.1 us
    pallas_call x1, Pallas kernels, gather(): pl.pallas_call(gather_kernel, out_shape=(jax.ShapeDtypeStruct(PIECES, BF1...  33.6 us
    pallas_call x1, Pallas kernels, attention(): pl.pallas_call(attention_kernel, out_shape=(jax.ShapeDtypeStruct(q.shape,...  11.1 us

profile of v2, /device:TPU:32, one launch (start us, length us, event | category | flops | bytes accessed | tf_op | source)
XLA Modules:
  0.0 88.3 jit_solution(16564358170271841569)
XLA Ops:
  0.6 33.6 %gather.1 = (bf16[4,2,4,2,128,256]{5,4,3,2,1,0:T(8,128)(2,1)}, bf16[128,1024]{1,0:T(8,128)(2,1)}) custom-call(bf16[128,128]{1,0:T(8,128)(2,1)} %k_ref.1, bf16[128,128]{1,0:T(8,128)(2,1)} %v_ref.1, bf16[32,4096]{1,0:T(8,128)(2,1)} %da_ref.1, bf16[1024,4096]{1,0:T(8,128)(2,1)} %w_ref.1), custom_call_target="tpu_custom_call" | custom-call | tf_op jit(solution)/shard_map/gather/pallas_call | solution.py:244
  34.2 11.1 %attention.1 = (bf16[128,1024]{1,0:T(8,128)(2,1)}, bf16[128,1024]{1,0:T(8,128)(2,1)}, bf16[8192,256]{1,0:T(8,128)(2,1)}) custom-call(s32[1]{0:T(128)} %bitcast.seq_ref, s32[128]{0:T(128)} %order_ref.1, s32[64,128]{1,0:T(8,128)} %bitcast.6, bf16[128,1024]{1,0:T(8,128)(2,1)} %q_ref.1, bf16[128,1024]{1,0:T(8,128)(2,1)} %get-tuple-element.9.g_ref, ...), custom_call_target="tpu_custom_call" | custom-call | tf_op jit(solution)/shard_map/attention/pallas_call | solution.py:426
  45.4 40.1 %scatter.1 = f32[128,256]{1,0:T(8,128)} custom-call(bf16[4,2,4,2,128,256]{5,4,3,2,1,0:T(8,128)(2,1)} %bitcast.5), custom_call_target="tpu_custom_call" | custom-call | tf_op jit(solution)/shard_map/scatter/pallas_call | solution.py:600
  85.4 1.5 %slice.12 = bf16[128,128]{1,0:T(8,128)(2,1)} slice(f32[128,256]{1,0:T(8,128)} %scatter.1), slice={[0:128], [128:256]} | slice | bytes 65536 | tf_op jit(solution)/shard_map/slice | solution.py:633
  86.9 1.5 %multiply_convert_fusion = bf16[128,128]{1,0:T(8,128)(2,1)} fusion(f32[128,256]{1,0:T(8,128)} %scatter.1), kind=kLoop, calls=%fused_computation.1 | loop fusion | flops 32768 | bytes 98304 | tf_op jit(solution)/shard_map/convert_element_type | solution.py:632

commit v3 on v2

--- a/solution.py
+++ b/solution.py
@@ -19,7 +19,6 @@
 SIZES = (4, 2, 1)
 CHUNK = 128
 PER_SUM = 8
-LOADS = 8
 MOST_KEYS = (65 + UNIT - 1) // UNIT * UNIT * SPAN
 SCALE = 1.0 / math.sqrt(D)
 EXP2_SCALE = SCALE * math.log2(math.e)
@@ -29,7 +28,8 @@
 VMEM = pl.BlockSpec(memory_space=pltpu.VMEM)
 SMEM = pl.BlockSpec(memory_space=pltpu.SMEM)
 ANY = pl.BlockSpec(memory_space=pl.ANY)
-LIMIT = 56 * 1024 * 1024
+MIB = 1024 * 1024
+GATHER_VMEM, ATTENTION_VMEM, SCATTER_VMEM = 54 * MIB, 34 * MIB, 8 * MIB
 PIECES = (4, 2, 4, 2, ROWS, 2 * D)
 
 
@@ -244,8 +244,8 @@
     return pl.pallas_call(
         gather_kernel,
         out_shape=(
-            jax.ShapeDtypeStruct(PIECES, BF16),
-            jax.ShapeDtypeStruct((ROWS, w.shape[0]), BF16),
+            pltpu.VMEM(PIECES, BF16),
+            pltpu.VMEM((ROWS, w.shape[0]), BF16),
         ),
         in_specs=[VMEM, VMEM, VMEM, ANY],
         out_specs=(ANY, VMEM),
@@ -262,25 +262,16 @@
             pltpu.SemaphoreType.DMA((4,)),
         ],
         compiler_params=pltpu.CompilerParams(
-            collective_id=0, has_side_effects=True, vmem_limit_bytes=LIMIT
+            collective_id=0, has_side_effects=True, vmem_limit_bytes=GATHER_VMEM
         ),
         name="gather",
     )(k, v, da, w)
 
 
 def attention_kernel(
-    seq_ref, order_ref, seg_ref, q_ref, g_ref, kv_ref, o_ref, dq_ref, dkv_ref,
-    kv, load_sem, stored, qs, gs, q_t, g_t, scores, weights, d_scores, acc,
+    seq_ref, order_ref, seg_ref, q_ref, g_ref, kv, o_ref, dq_ref, dkv_ref,
+    stored, qs, gs, q_t, g_t, scores, weights, d_scores, acc,
 ):
-    chunk = TOKENS // LOADS
-    loads = [
-        pltpu.make_async_copy(
-            kv_ref.at[pl.ds(c * chunk, chunk)], kv.at[pl.ds(c * chunk, chunk)], load_sem.at[c]
-        )
-        for c in range(LOADS)
-    ]
-    for copy in loads:
-        copy.start()
     seq = seq_ref[0]
     for r in range(SPANS):
         stored[order_ref[r]] = r
@@ -295,9 +286,6 @@
         for start in starts:
             first = jnp.maximum(first, jnp.where(start <= position, start, 0))
         return first
-
-    for copy in loads:
-        copy.wait()
 
     def one_span(half, _):
         row = pl.multiple_of(half * SPAN, SPAN)
@@ -430,11 +418,9 @@
             jax.ShapeDtypeStruct(q.shape, BF16),
             jax.ShapeDtypeStruct(kv.shape, BF16),
         ),
-        in_specs=[SMEM, SMEM, VMEM, VMEM, VMEM, ANY],
+        in_specs=[SMEM, SMEM, VMEM, VMEM, VMEM, VMEM],
         out_specs=(VMEM, VMEM, VMEM),
         scratch_shapes=[
-            pltpu.VMEM(kv.shape, BF16),
-            pltpu.SemaphoreType.DMA((LOADS,)),
             pltpu.SMEM((SPANS,), jnp.int32),
             pltpu.VMEM((QROWS, D), BF16),
             pltpu.VMEM((QROWS, D), BF16),
@@ -445,7 +431,7 @@
             pltpu.VMEM((max(SIZES) * UNIT * SPAN, QROWS), BF16),
             pltpu.VMEM((D, QROWS), F32),
         ],
-        compiler_params=pltpu.CompilerParams(vmem_limit_bytes=LIMIT),
+        compiler_params=pltpu.CompilerParams(vmem_limit_bytes=ATTENTION_VMEM),
         name="attention",
     )(seq, order, seg, q, g, kv)
 
@@ -613,10 +599,26 @@
             pltpu.SemaphoreType.DMA((12,)),
         ],
         compiler_params=pltpu.CompilerParams(
-            collective_id=1, has_side_effects=True, vmem_limit_bytes=LIMIT
+            collective_id=1, has_side_effects=True, vmem_limit_bytes=SCATTER_VMEM
         ),
         name="scatter",
     )(part)
+
+
+def finish_kernel(sum_ref, dk_ref, dv_ref):
+    dk_ref[...] = (sum_ref[:, :D] * SCALE).astype(BF16)
+    dv_ref[...] = sum_ref[:, D:].astype(BF16)
+
+
+def finish(sums):
+    return pl.pallas_call(
+        finish_kernel,
+        out_shape=(jax.ShapeDtypeStruct((ROWS, D), BF16),) * 2,
+        in_specs=[VMEM],
+        out_specs=(VMEM, VMEM),
+        compiler_params=pltpu.CompilerParams(vmem_limit_bytes=2 * MIB),
+        name="finish",
+    )(sums)
 
 
 def shards(
@@ -629,8 +631,7 @@
         pieces.reshape(TOKENS, 2 * D),
     )
     sums = scatter(terms.reshape(PIECES))
-    key_gradient = (sums[:, :D] * SCALE).astype(BF16)
-    value_gradient = sums[:, D:].astype(BF16)
+    key_gradient, value_gradient = finish(sums)
     return (attended, d_queries, key_gradient, value_gradient)
 
 

time: 88.6 us -> 78.5 us (0.89)
  Pallas kernels: 84.8 us -> 77.7 us
  other arithmetic: 1.46 us -> 0 us
  local copies, waits for them, and re-layouts: 1.46 us -> 0.01 us
    pallas_call x1, Pallas kernels: 11.1 us -> 7.3 us  [attention(): pl.pallas_call(attention_kernel, out_shape=(jax.ShapeDtypeStruct(q.shape,...]
    pallas_call x1, Pallas kernels: 40.1 us -> 37.6 us  [scatter(): pl.pallas_call(scatter_kernel, out_shape=jax.ShapeDtypeStruct((ROWS, 2 *...]
    convert_element_type x1 -> x0, other arithmetic: 1.46 us -> none  [shards(): key_gradient = (sums[:, :D] * SCALE).astype(BF16)]
    slice x1 -> x0, local copies, waits for them, and re-layouts: 1.46 us -> none  [shards(): value_gradient = sums[:, D:].astype(BF16)]
    pallas_call x1 -> x2, Pallas kernels: 33.6 us -> 32.8 us  [the longest x1 32.1 us: gather(): pl.pallas_call(gather_kernel, out_shape=(pltpu.VMEM(PIECES, BF16), pltpu....]
where the time goes in v3:
time: 78.5 us; the launch traced here: 78.4 us
  Pallas kernels  77.7 us (99%)
    pallas_call x1, Pallas kernels, scatter(): pl.pallas_call(scatter_kernel, out_shape=jax.ShapeDtypeStruct((ROWS, 2 *...  37.6 us
    pallas_call x1, Pallas kernels, gather(): pl.pallas_call(gather_kernel, out_shape=(pltpu.VMEM(PIECES, BF16), pltpu....  32.1 us
    pallas_call x1, Pallas kernels, attention(): pl.pallas_call(attention_kernel, out_shape=(jax.ShapeDtypeStruct(q.shape,...  7.3 us

profile of v3, /device:TPU:32, one launch (start us, length us, event | category | flops | bytes accessed | tf_op | source)
XLA Modules:
  0.0 78.4 jit_solution(4877939704227313338)
XLA Ops:
  0.6 0.0 copy-start
  0.6 0.0 copy-start.1
  0.7 0.0 copy-start.2
  0.7 32.1 %gather.1 = (bf16[4,2,4,2,128,256]{5,4,3,2,1,0:T(8,128)(2,1)S(1)}, bf16[128,1024]{1,0:T(8,128)(2,1)S(1)}) custom-call(bf16[128,128]{1,0:T(8,128)(2,1)} %k_ref.1, bf16[128,128]{1,0:T(8,128)(2,1)} %v_ref.1, bf16[32,4096]{1,0:T(8,128)(2,1)} %da_ref.1, bf16[1024,4096]{1,0:T(8,128)(2,1)} %w_ref.1), custom_call_target="tpu_custom_call" | custom-call | tf_op jit(solution)/shard_map/gather/pallas_call | solution.py:244
  32.8 0.0 copy-done
  32.8 0.0 copy-done.1
  32.8 0.0 copy-done.2
  32.9 7.3 %attention.1 = (bf16[128,1024]{1,0:T(8,128)(2,1)}, bf16[128,1024]{1,0:T(8,128)(2,1)}, bf16[8192,256]{1,0:T(8,128)(2,1)S(1)}) custom-call(s32[1]{0:T(128)} %bitcast.seq_ref, s32[128]{0:T(128)S(1)} %copy-done.2, s32[64,128]{1,0:T(8,128)S(1)} %bitcast.6, bf16[128,1024]{1,0:T(8,128)(2,1)S(1)} %copy-done, bf16[128,1024]{1,0:T(8,128)(2,1)S(1)} %get-tuple-element.11.g_ref, ...), custom_call_target="tpu_custom_call" | custom-call | tf_op jit(solution)/shard_map/attention/pallas_call | solution.py:414
  40.2 37.6 %scatter.1.sum_ref = f32[128,256]{1,0:T(8,128)S(1)} custom-call(bf16[4,2,4,2,128,256]{5,4,3,2,1,0:T(8,128)(2,1)S(1)} %bitcast.5), custom_call_target="tpu_custom_call" | custom-call | tf_op jit(solution)/shard_map/scatter/pallas_call | solution.py:586
  77.8 0.6 finish.1
Async XLA Ops:
  0.6 32.2 %copy-start = (bf16[128,1024]{1,0:T(8,128)(2,1)S(1)}, bf16[128,1024]{1,0:T(8,128)(2,1)}, u32[]{:S(2)}) copy-start(bf16[128,1024]{1,0:T(8,128)(2,1)} %q_ref.1) | copy-start | bytes 786436
  0.6 32.2 %copy-start.1 = (s32[8192]{0:T(1024)S(1)}, s32[8192]{0:T(1024)}, u32[]{:S(2)}) copy-start(s32[8192]{0:T(1024)} %param.10) | copy-start | bytes 98308
  0.7 32.2 %copy-start.2 = (s32[128]{0:T(128)S(1)}, s32[128]{0:T(128)}, u32[]{:S(2)}) copy-start(s32[128]{0:T(128)} %order_ref.1) | copy-start | bytes 1540

commit v4 on v3

--- a/solution.py
+++ b/solution.py
@@ -18,7 +18,7 @@
 UNIT = 8
 SIZES = (4, 2, 1)
 CHUNK = 128
-PER_SUM = 8
+PER_MIX, PER_SUM, SLOPE = 8, 8, 512
 MOST_KEYS = (65 + UNIT - 1) // UNIT * UNIT * SPAN
 SCALE = 1.0 / math.sqrt(D)
 EXP2_SCALE = SCALE * math.log2(math.e)
@@ -141,30 +141,20 @@
         arrived(da_all.at[far, :, pl.ds(half, half)], x_send.at[0], x_recv.at[3], mate)
         w_copy.wait()
 
-    def product(at):
+    def product(step, _):
         width = 256
+        at = pl.ds(pl.multiple_of(step * width, width), width)
         rows = da_all[...].reshape(ROWS, da_ref.shape[1])
-        g_ref[:, at * width:(at + 1) * width] = lax.dot_general(
-            rows, w_all[at * width:(at + 1) * width, :], (((1,), (1,)), ((), ())),
-            preferred_element_type=F32,
+        g_ref[:, at] = lax.dot_general(
+            rows, w_all[at, :], (((1,), (1,)), ((), ())), preferred_element_type=F32
         ).astype(BF16)
+        return 0
 
     def to_mate(src, dst):
         pltpu.make_async_remote_copy(
             src_ref=src, dst_ref=dst, send_sem=mate_send, recv_sem=mate_recv,
             device_id=mate, device_id_type=MESH,
         ).start()
-
-    def finish(core, sends):
-        theirs = kv_ref.at[:, :, :, 1 - core]
-        ours = kv_ref.at[:, :, :, core]
-        arrived(theirs, mate_send, mate_recv, mate)
-        pltpu.make_async_remote_copy(
-            src_ref=ours, dst_ref=ours, send_sem=mate_send, recv_sem=mate_recv,
-            device_id=mate, device_id_type=MESH,
-        ).wait_send()
-        sends.wait()
-        x_sends.wait()
 
     up_z, down_z = me.device(z=me.dz(1)), me.device(z=me.dz(-1))
     up_2z, down_2z = me.device(z=me.dz(2)), me.device(z=me.dz(-2))
@@ -195,48 +185,54 @@
         for i in (0, 1, -1, 2):
             fetch(0, sends, i, -2, [up_2z, up_z] if i in (0, 1) else [up_z])
             fetch(0, sends, i, 2, [down_2z, down_z] if i in (-1, 2) else [down_z])
-        x_end()
-        for at, i in enumerate((0, 1, -1, 2)):
-            product(at)
+        for i in (0, 1, -1, 2):
             fetch(0, sends, i, -3, [])
             fetch(0, sends, i, 3, [])
         for i in (0, -1, 1, 2):
             fetch(0, sends, i, 4, [])
-        finish(0, sends)
+        sends.wait()
+        x_sends.wait()
 
     @pl.when(me.core == 1)
     def _():
         sends = Sends(send_sem)
-        fetch(1, sends, 0, 0, [up_z, down_z, up_2z, down_2z, up_y, down_y], wait=False)
+        ys = [up_y, down_y]
+        fetch(1, sends, 0, 0, [up_z, down_z, up_2z, down_2z] + ys, wait=False)
         x_start()
 
         def across(s):
             fetch(1, sends, -1, s, [up_y] if s <= 0 else [])
             fetch(1, sends, 1, s, [down_y] if s > 0 else [])
 
-        fetch(1, sends, 0, -1, [up_y, down_y])
-        fetch(1, sends, 0, 1, [up_y, down_y])
+        fetch(1, sends, 0, -1, ys)
+        fetch(1, sends, 0, 1, ys)
         across(0)
-        fetch(1, sends, 0, -2, [up_2z, up_z, up_y, down_y])
-        fetch(1, sends, 0, 2, [down_z, up_y, down_y])
+        fetch(1, sends, 0, -2, [up_2z, up_z] + ys)
+        fetch(1, sends, 0, 2, [down_z] + ys)
         across(-1)
         across(1)
-        fetch(1, sends, 0, -3, [up_y, down_y])
-        fetch(1, sends, 0, 3, [up_y, down_y])
+        fetch(1, sends, 0, -3, ys)
+        fetch(1, sends, 0, 3, ys)
         across(-2)
         across(2)
-        fetch(1, sends, 0, 4, [up_y, down_y])
+        fetch(1, sends, 0, 4, ys)
         x_middle()
-        across(-3)
-        across(3)
-        across(4)
-        x_end()
-        for at in range(4):
-            product(at)
-            for s in ((0, -1), (1, -2), (2, -3), (3, 4))[at]:
-                fetch(1, sends, 2, s, [])
-        finish(1, sends)
-
+        for s in (-3, 3, 4):
+            across(s)
+        for s in (0, -1, 1, -2, 2, -3, 3, 4):
+            fetch(1, sends, 2, s, [])
+        sends.wait()
+        x_sends.wait()
+
+    x_end()
+    lax.fori_loop(0, g_ref.shape[1] // 256, product, 0)
+    theirs = kv_ref.at[:, :, :, 1 - me.core]
+    ours = kv_ref.at[:, :, :, me.core]
+    arrived(theirs, mate_send, mate_recv, mate)
+    pltpu.make_async_remote_copy(
+        src_ref=ours, dst_ref=ours, send_sem=mate_send, recv_sem=mate_recv,
+        device_id=mate, device_id_type=MESH,
+    ).wait_send()
     own_copy.wait()
 
 
@@ -349,15 +345,21 @@
         acc[...] = jnp.zeros_like(acc)
 
         def forward(at, count, total):
-            for c in range(count // per):
-                part = keys(at, c * CHUNK, CHUNK)
-                exponent = jnp.exp2(scores[part, :] * EXP2_SCALE - top)
-                weights[part, :] = exponent.astype(BF16)
-                total = total + jnp.sum(exponent.reshape(CHUNK // 8, 8, QROWS), axis=0)
-            acc[...] += lax.dot_general(
-                load(rows_of(at, count), 1), weights[keys(at, 0, count * SPAN), :],
-                (((0,), (0,)), ((), ())), preferred_element_type=F32,
-            )
+            rows = rows_of(at, count)
+            for u in range(count // PER_MIX):
+                parts = []
+                for c in range(u * PER_MIX // per, (u + 1) * PER_MIX // per):
+                    part = keys(at, c * CHUNK, CHUNK)
+                    exponent = jnp.exp2(scores[part, :] * EXP2_SCALE - top)
+                    rounded = exponent.astype(BF16)
+                    weights[part, :] = rounded
+                    parts.append(rounded)
+                    total = total + jnp.sum(exponent.reshape(CHUNK // 8, 8, QROWS), axis=0)
+                acc[...] += lax.dot_general(
+                    load(rows[u * PER_MIX:(u + 1) * PER_MIX], 1),
+                    jnp.concatenate(parts, axis=0),
+                    (((0,), (0,)), ((), ())), preferred_element_type=F32,
+                )
             return total
 
         total = tiles(forward, jnp.zeros((8, QROWS), F32))
@@ -376,12 +378,13 @@
 
         def backward(at, count, carried):
             rows = rows_of(at, count)
-            for c in range(count // per):
+            step = SLOPE // SPAN
+            for c in range(count // step):
                 d_prob = jnp.dot(
-                    load(rows[c * per:(c + 1) * per], 1), g_t[...], preferred_element_type=F32
+                    load(rows[c * step:(c + 1) * step], 1), g_t[...], preferred_element_type=F32
                 )
-                weight = weights[keys(at, c * CHUNK, CHUNK), :].astype(F32)
-                d_scores[c * CHUNK:(c + 1) * CHUNK, :] = (weight * (d_prob - delta)).astype(BF16)
+                weight = weights[keys(at, c * SLOPE, SLOPE), :].astype(F32)
+                d_scores[c * SLOPE:(c + 1) * SLOPE, :] = (weight * (d_prob - delta)).astype(BF16)
             acc[...] += lax.dot_general(
                 load(rows, 0), d_scores[:count * SPAN, :], (((0,), (0,)), ((), ())),
                 preferred_element_type=F32,
@@ -436,8 +439,8 @@
     )(seq, order, seg, q, g, kv)
 
 
+SUM_ROWS = 32
 FAR_FIRST = (4, 3, -3, 2, -2, 1, -1, 0)
-UPWARD = (4, -3, 2, -1)
 
 
 def scatter_kernel(
@@ -479,17 +482,30 @@
     up_y, down_y = me.device(y=me.dy(1)), me.device(y=me.dy(-1))
     index = FAR_FIRST.index
 
-    def terms(py, pz, slots):
+    def terms(py, pz, slots, store):
         at = (py,) + pz[1:]
-        total = mine[at].astype(F32) + theirs[at].astype(F32)
         for slot in slots:
             arrived(landed.at[slot], mate_send.at[0], recv_sem.at[slot], mate)
-            total = total + landed[slot].astype(F32)
-        return at, total
+
+        def add(step, _):
+            rows = pl.ds(pl.multiple_of(step * SUM_ROWS, SUM_ROWS), SUM_ROWS)
+            total = mine[at + (rows,)].astype(F32) + theirs[at + (rows,)].astype(F32)
+            for slot in slots:
+                total = total + landed[slot, rows].astype(F32)
+            store(at, rows, total)
+            return 0
+
+        lax.fori_loop(0, ROWS // SUM_ROWS, add, 0)
+        return at
+
+    def keep(at, rows, total):
+        mine[at + (rows,)] = total.astype(BF16)
+
+    def write(at, rows, total):
+        sum_ref[rows, :] = total
 
     def pass_on(sends, py, pz, slots, slot, device):
-        at, total = terms(py, pz, slots)
-        mine[at] = total.astype(BF16)
+        at = terms(py, pz, slots, keep)
         sends(mine.at[at], landed.at[slot], recv_sem.at[slot], device)
 
     @pl.when(me.core == 0)
@@ -529,13 +545,12 @@
                 got += (down_slot(4, i),) if s == 2 and i in (-1, 2) else ()
                 pass_on(sends, me.dy(i), me.dz(-s), got, down_slot(s, i), down_z)
         ready(0)
+        last = lambda i: (up_slot(1, i), down_slot(1, i))
         for i in (1, -1, 2):
             pass_on(
-                sends, me.dy(i), z, (up_slot(1, i), down_slot(1, i)),
-                32 + order.index(i), me.device(y=me.dy(i)),
+                sends, me.dy(i), z, last(i), 32 + order.index(i), me.device(y=me.dy(i))
             )
-        _, total = terms(y, z, (up_slot(1, 0), down_slot(1, 0), 33, 34, 35))
-        sum_ref[...] = total
+        terms(y, z, last(0) + (33, 34, 35), write)
         mate_sends.wait()
         sends.wait()
 
@@ -556,16 +571,12 @@
         for s in FAR_FIRST:
             at = (me.dy(2),) + me.dz(s)[1:]
             arrived(theirs.at[at], mate_send.at[0], mate_recv.at[4 + index(s)], mate)
-            if s in UPWARD:
-                pass_on(sends, me.dy(2), me.dz(s), (), index(s), up_y)
-            else:
-                pass_on(sends, me.dy(2), me.dz(s), (), index(s), down_y)
+            pass_on(sends, me.dy(2), me.dz(s), (), index(s), me.device(y=me.dy(2)))
         ready(1)
         ready(-1)
         for s in FAR_FIRST:
-            got = (index(s),)
-            pass_on(sends, me.dy(1), me.dz(s), got if s in UPWARD else (), 8 + index(s), up_y)
-            pass_on(sends, me.dy(-1), me.dz(s), () if s in UPWARD else got, 16 + index(s), down_y)
+            pass_on(sends, me.dy(1), me.dz(s), (), 8 + index(s), up_y)
+            pass_on(sends, me.dy(-1), me.dz(s), (), 16 + index(s), down_y)
         ready(0)
         routes = {
             4: ((), up_2z), 3: ((), up_z), -3: ((), down_z), 2: ((3, 4), up_2z),
@@ -573,11 +584,10 @@
         }
         for s in FAR_FIRST[:-1]:
             extra, device = routes[s]
-            got = (8 + index(s), 16 + index(s)) + tuple(24 + index(e) for e in extra)
+            got = (index(s), 8 + index(s), 16 + index(s)) + tuple(24 + index(e) for e in extra)
             pass_on(sends, y, me.dz(s), got, 24 + index(s), device)
-        got = (15, 23) + tuple(24 + index(e) for e in (1, -1, 2, -2))
-        _, total = terms(y, z, got)
-        sum_ref[...] = total
+        got = (7, 15, 23) + tuple(24 + index(e) for e in (1, -1, 2, -2))
+        terms(y, z, got, write)
         mate_sends.wait()
         sends.wait()
 

time: 78.5 us -> 78.4 us (level)
    pallas_call x1, Pallas kernels: 7.3 us -> 11.9 us  [attention(): pl.pallas_call(attention_kernel, out_shape=(jax.ShapeDtypeStruct(q.shape,...]
    pallas_call x1, Pallas kernels: 37.6 us -> 33.6 us  [scatter(): pl.pallas_call(scatter_kernel, out_shape=jax.ShapeDtypeStruct((ROWS, 2 *...]
where the time goes in v4:
time: 78.4 us; the launch traced here: 78.3 us
  Pallas kernels  77.6 us (99%)
    pallas_call x1, Pallas kernels, scatter(): pl.pallas_call(scatter_kernel, out_shape=jax.ShapeDtypeStruct((ROWS, 2 *...  33.6 us
    pallas_call x1, Pallas kernels, gather(): pl.pallas_call(gather_kernel, out_shape=(pltpu.VMEM(PIECES, BF16), pltpu....  31.4 us
    pallas_call x1, Pallas kernels, attention(): pl.pallas_call(attention_kernel, out_shape=(jax.ShapeDtypeStruct(q.shape,...  11.9 us

profile of v4, /device:TPU:32, one launch (start us, length us, event | category | flops | bytes accessed | tf_op | source)
XLA Modules:
  0.0 78.3 jit_solution(17723761767637180386)
XLA Ops:
  0.6 0.0 copy-start
  0.6 0.0 copy-start.1
  0.7 0.0 copy-start.2
  0.7 31.4 %gather.1 = (bf16[4,2,4,2,128,256]{5,4,3,2,1,0:T(8,128)(2,1)S(1)}, bf16[128,1024]{1,0:T(8,128)(2,1)S(1)}) custom-call(bf16[128,128]{1,0:T(8,128)(2,1)} %k_ref.1, bf16[128,128]{1,0:T(8,128)(2,1)} %v_ref.1, bf16[32,4096]{1,0:T(8,128)(2,1)} %da_ref.1, bf16[1024,4096]{1,0:T(8,128)(2,1)} %w_ref.1), custom_call_target="tpu_custom_call" | custom-call | tf_op jit(solution)/shard_map/gather/pallas_call | solution.py:240
  32.1 0.0 copy-done
  32.1 0.0 copy-done.1
  32.1 0.0 copy-done.2
  32.1 11.9 %attention.1 = (bf16[128,1024]{1,0:T(8,128)(2,1)}, bf16[128,1024]{1,0:T(8,128)(2,1)}, bf16[8192,256]{1,0:T(8,128)(2,1)S(1)}) custom-call(s32[1]{0:T(128)} %bitcast.seq_ref, s32[128]{0:T(128)S(1)} %copy-done.2, s32[64,128]{1,0:T(8,128)S(1)} %bitcast.6, bf16[128,1024]{1,0:T(8,128)(2,1)S(1)} %copy-done, bf16[128,1024]{1,0:T(8,128)(2,1)S(1)} %get-tuple-element.11.g_ref, ...), custom_call_target="tpu_custom_call" | custom-call | tf_op jit(solution)/shard_map/attention/pallas_call | solution.py:417
  44.1 33.6 %scatter.1.sum_ref = f32[128,256]{1,0:T(8,128)S(1)} custom-call(bf16[4,2,4,2,128,256]{5,4,3,2,1,0:T(8,128)(2,1)S(1)} %bitcast.5), custom_call_target="tpu_custom_call" | custom-call | tf_op jit(solution)/shard_map/scatter/pallas_call | solution.py:596
  77.7 0.6 finish.1
Async XLA Ops:
  0.6 31.5 %copy-start = (bf16[128,1024]{1,0:T(8,128)(2,1)S(1)}, bf16[128,1024]{1,0:T(8,128)(2,1)}, u32[]{:S(2)}) copy-start(bf16[128,1024]{1,0:T(8,128)(2,1)} %q_ref.1) | copy-start | bytes 786436
  0.6 31.5 %copy-start.1 = (s32[8192]{0:T(1024)S(1)}, s32[8192]{0:T(1024)}, u32[]{:S(2)}) copy-start(s32[8192]{0:T(1024)} %param.10) | copy-start | bytes 98308
  0.7 31.5 %copy-start.2 = (s32[128]{0:T(128)S(1)}, s32[128]{0:T(128)}, u32[]{:S(2)}) copy-start(s32[128]{0:T(128)} %order_ref.1) | copy-start | bytes 1540

commit v5 on v3

--- a/solution.py
+++ b/solution.py
@@ -18,7 +18,7 @@
 UNIT = 8
 SIZES = (4, 2, 1)
 CHUNK = 128
-PER_SUM = 8
+PER_MIX, PER_SUM, SLOPE = 8, 8, 512
 MOST_KEYS = (65 + UNIT - 1) // UNIT * UNIT * SPAN
 SCALE = 1.0 / math.sqrt(D)
 EXP2_SCALE = SCALE * math.log2(math.e)
@@ -349,15 +349,21 @@
         acc[...] = jnp.zeros_like(acc)
 
         def forward(at, count, total):
-            for c in range(count // per):
-                part = keys(at, c * CHUNK, CHUNK)
-                exponent = jnp.exp2(scores[part, :] * EXP2_SCALE - top)
-                weights[part, :] = exponent.astype(BF16)
-                total = total + jnp.sum(exponent.reshape(CHUNK // 8, 8, QROWS), axis=0)
-            acc[...] += lax.dot_general(
-                load(rows_of(at, count), 1), weights[keys(at, 0, count * SPAN), :],
-                (((0,), (0,)), ((), ())), preferred_element_type=F32,
-            )
+            rows = rows_of(at, count)
+            for u in range(count // PER_MIX):
+                parts = []
+                for c in range(u * PER_MIX // per, (u + 1) * PER_MIX // per):
+                    part = keys(at, c * CHUNK, CHUNK)
+                    exponent = jnp.exp2(scores[part, :] * EXP2_SCALE - top)
+                    rounded = exponent.astype(BF16)
+                    weights[part, :] = rounded
+                    parts.append(rounded)
+                    total = total + jnp.sum(exponent.reshape(CHUNK // 8, 8, QROWS), axis=0)
+                acc[...] += lax.dot_general(
+                    load(rows[u * PER_MIX:(u + 1) * PER_MIX], 1),
+                    jnp.concatenate(parts, axis=0),
+                    (((0,), (0,)), ((), ())), preferred_element_type=F32,
+                )
             return total
 
         total = tiles(forward, jnp.zeros((8, QROWS), F32))
@@ -376,12 +382,13 @@
 
         def backward(at, count, carried):
             rows = rows_of(at, count)
-            for c in range(count // per):
+            step = SLOPE // SPAN
+            for c in range(count // step):
                 d_prob = jnp.dot(
-                    load(rows[c * per:(c + 1) * per], 1), g_t[...], preferred_element_type=F32
+                    load(rows[c * step:(c + 1) * step], 1), g_t[...], preferred_element_type=F32
                 )
-                weight = weights[keys(at, c * CHUNK, CHUNK), :].astype(F32)
-                d_scores[c * CHUNK:(c + 1) * CHUNK, :] = (weight * (d_prob - delta)).astype(BF16)
+                weight = weights[keys(at, c * SLOPE, SLOPE), :].astype(F32)
+                d_scores[c * SLOPE:(c + 1) * SLOPE, :] = (weight * (d_prob - delta)).astype(BF16)
             acc[...] += lax.dot_general(
                 load(rows, 0), d_scores[:count * SPAN, :], (((0,), (0,)), ((), ())),
                 preferred_element_type=F32,
@@ -436,8 +443,11 @@
     )(seq, order, seg, q, g, kv)
 
 
+SUM_ROWS = 32
+SPLIT = 64
 FAR_FIRST = (4, 3, -3, 2, -2, 1, -1, 0)
 UPWARD = (4, -3, 2, -1)
+Z_SLOTS = 36
 
 
 def scatter_kernel(
@@ -479,23 +489,73 @@
     up_y, down_y = me.device(y=me.dy(1)), me.device(y=me.dy(-1))
     index = FAR_FIRST.index
 
-    def terms(py, pz, slots):
-        at = (py,) + pz[1:]
-        total = mine[at].astype(F32) + theirs[at].astype(F32)
-        for slot in slots:
-            arrived(landed.at[slot], mate_send.at[0], recv_sem.at[slot], mate)
-            total = total + landed[slot].astype(F32)
-        return at, total
-
-    def pass_on(sends, py, pz, slots, slot, device):
-        at, total = terms(py, pz, slots)
-        mine[at] = total.astype(BF16)
-        sends(mine.at[at], landed.at[slot], recv_sem.at[slot], device)
+    def keep(at, rows, total):
+        mine[at + (rows,)] = total.astype(BF16)
+
+    def write(at, rows, total):
+        sum_ref[rows, :] = total
+
+    class Route:
+        def __init__(self, sends, start, size, first_sem):
+            self.sends, self.start, self.size, self.first_sem = sends, start, size, first_sem
+
+        def slot(self, slot):
+            return landed.at[slot, pl.ds(self.start, self.size)]
+
+        def terms(self, py, pz, slots, store):
+            at = (py,) + pz[1:]
+            for slot in slots:
+                arrived(
+                    self.slot(slot), mate_send.at[0], recv_sem.at[self.first_sem + slot], mate
+                )
+
+            def add(step, _):
+                first = pl.multiple_of(self.start + step * SUM_ROWS, SUM_ROWS)
+                rows = pl.ds(first, SUM_ROWS)
+                total = mine[at + (rows,)].astype(F32) + theirs[at + (rows,)].astype(F32)
+                for slot in slots:
+                    total = total + landed[slot, rows].astype(F32)
+                store(at, rows, total)
+                return 0
+
+            lax.fori_loop(0, self.size // SUM_ROWS, add, 0)
+            return at
+
+        def pass_on(self, py, pz, slots, slot, device):
+            at = self.terms(py, pz, slots, keep)
+            self.sends(
+                mine.at[at + (pl.ds(self.start, self.size),)], self.slot(slot),
+                recv_sem.at[self.first_sem + slot], device,
+            )
+
+    def y_far(route, s):
+        device = up_y if s in UPWARD else down_y
+        route.pass_on(me.dy(2), me.dz(s), (), index(s), device)
+
+    def y_near(route, s):
+        got = (index(s),)
+        up, down = (got, ()) if s in UPWARD else ((), got)
+        route.pass_on(me.dy(1), me.dz(s), up, 8 + index(s), up_y)
+        route.pass_on(me.dy(-1), me.dz(s), down, 16 + index(s), down_y)
+
+    def along_z(route, s):
+        extra, device = {
+            4: ((), up_2z), 3: ((), up_z), -3: ((), down_z), 2: ((3, 4), up_2z),
+            -2: ((-3,), down_2z), 1: ((), up_z), -1: ((), down_z),
+        }[s]
+        got = (8 + index(s), 16 + index(s)) + tuple(24 + index(e) for e in extra)
+        route.pass_on(y, me.dz(s), got, 24 + index(s), device)
+
+    def y_last(route):
+        got = (15, 23) + tuple(24 + index(e) for e in (1, -1, 2, -2))
+        route.terms(y, z, got, write)
 
     @pl.when(me.core == 0)
     def _():
         sends = Sends(send_sem)
         mate_sends = Sends(mate_send)
+        by_z = Route(sends, 0, SPLIT, 0)
+        by_y = Route(sends, SPLIT, ROWS - SPLIT, Z_SLOTS)
         for s in FAR_FIRST:
             at = (me.dy(2),) + me.dz(s)[1:]
             mate_sends(
@@ -512,30 +572,54 @@
         order = (0, 1, -1, 2)
         up_slot = lambda s, i: (s - 1) * 4 + order.index(i)
         down_slot = lambda s, i: 16 + (s - 1) * 4 + order.index(i)
+
+        def z_step(s):
+            for i in order:
+                got = (up_slot(s + 1, i),) if s < 3 else ()
+                got += (up_slot(4, i),) if s == 2 and i in (0, 1) else ()
+                by_z.pass_on(me.dy(i), me.dz(s), got, up_slot(s, i), up_z)
+                got = (down_slot(s + 1, i),) if s < 3 else ()
+                got += (down_slot(4, i),) if s == 2 and i in (-1, 2) else ()
+                by_z.pass_on(me.dy(i), me.dz(-s), got, down_slot(s, i), down_z)
+
         ready(4)
         for i in (0, -1, 1, 2):
             if i in (0, 1):
-                pass_on(sends, me.dy(i), me.dz(4), (), up_slot(4, i), up_2z)
+                by_z.pass_on(me.dy(i), me.dz(4), (), up_slot(4, i), up_2z)
             else:
-                pass_on(sends, me.dy(i), me.dz(4), (), down_slot(4, i), down_2z)
-        for s in (3, 2, 1):
-            ready(s)
-            ready(-s)
-            for i in order:
-                got = (up_slot(s + 1, i),) if s < 3 else ()
-                got += (up_slot(4, i),) if s == 2 and i in (0, 1) else ()
-                pass_on(sends, me.dy(i), me.dz(s), got, up_slot(s, i), up_z)
-                got = (down_slot(s + 1, i),) if s < 3 else ()
-                got += (down_slot(4, i),) if s == 2 and i in (-1, 2) else ()
-                pass_on(sends, me.dy(i), me.dz(-s), got, down_slot(s, i), down_z)
+                by_z.pass_on(me.dy(i), me.dz(4), (), down_slot(4, i), down_2z)
+        y_far(by_y, 4)
+        ready(3)
+        ready(-3)
+        z_step(3)
+        for s in (3, -3):
+            y_far(by_y, s)
+        ready(2)
+        ready(-2)
+        for s in (2, -2):
+            y_far(by_y, s)
+        y_near(by_y, 4)
+        z_step(2)
+        ready(1)
+        ready(-1)
+        for s in (1, -1):
+            y_far(by_y, s)
+        for s in (3, -3):
+            y_near(by_y, s)
         ready(0)
+        y_far(by_y, 0)
+        z_step(1)
+        for s in (2, -2, 1, -1, 0):
+            y_near(by_y, s)
+        for s in (4, 3, -3):
+            along_z(by_y, s)
+        last = lambda i: (up_slot(1, i), down_slot(1, i))
         for i in (1, -1, 2):
-            pass_on(
-                sends, me.dy(i), z, (up_slot(1, i), down_slot(1, i)),
-                32 + order.index(i), me.device(y=me.dy(i)),
-            )
-        _, total = terms(y, z, (up_slot(1, 0), down_slot(1, 0), 33, 34, 35))
-        sum_ref[...] = total
+            by_z.pass_on(me.dy(i), z, last(i), 32 + order.index(i), me.device(y=me.dy(i)))
+        for s in (1, -1, 2, -2):
+            along_z(by_y, s)
+        by_z.terms(y, z, last(0) + (33, 34, 35), write)
+        y_last(by_y)
         mate_sends.wait()
         sends.wait()
 
@@ -543,6 +627,7 @@
     def _():
         sends = Sends(send_sem)
         mate_sends = Sends(mate_send)
+        by_y = Route(sends, 0, ROWS, Z_SLOTS)
         for s in FAR_FIRST:
             at = of_z(s)
             mate_sends(part_ref.at[at + (0,)], theirs.at[at], mate_recv.at[me.dz(s)[0]], mate)
@@ -556,28 +641,15 @@
         for s in FAR_FIRST:
             at = (me.dy(2),) + me.dz(s)[1:]
             arrived(theirs.at[at], mate_send.at[0], mate_recv.at[4 + index(s)], mate)
-            if s in UPWARD:
-                pass_on(sends, me.dy(2), me.dz(s), (), index(s), up_y)
-            else:
-                pass_on(sends, me.dy(2), me.dz(s), (), index(s), down_y)
+            y_far(by_y, s)
         ready(1)
         ready(-1)
         for s in FAR_FIRST:
-            got = (index(s),)
-            pass_on(sends, me.dy(1), me.dz(s), got if s in UPWARD else (), 8 + index(s), up_y)
-            pass_on(sends, me.dy(-1), me.dz(s), () if s in UPWARD else got, 16 + index(s), down_y)
+            y_near(by_y, s)
         ready(0)
-        routes = {
-            4: ((), up_2z), 3: ((), up_z), -3: ((), down_z), 2: ((3, 4), up_2z),
-            -2: ((-3,), down_2z), 1: ((), up_z), -1: ((), down_z),
-        }
         for s in FAR_FIRST[:-1]:
-            extra, device = routes[s]
-            got = (8 + index(s), 16 + index(s)) + tuple(24 + index(e) for e in extra)
-            pass_on(sends, y, me.dz(s), got, 24 + index(s), device)
-        got = (15, 23) + tuple(24 + index(e) for e in (1, -1, 2, -2))
-        _, total = terms(y, z, got)
-        sum_ref[...] = total
+            along_z(by_y, s)
+        y_last(by_y)
         mate_sends.wait()
         sends.wait()
 
@@ -593,8 +665,8 @@
             pltpu.VMEM((4, 2, 4, ROWS, 2 * D), BF16),
             pltpu.VMEM((36, ROWS, 2 * D), BF16),
             pltpu.SemaphoreType.DMA((8,)),
-            pltpu.SemaphoreType.DMA((40,)),
-            pltpu.SemaphoreType.DMA((36,)),
+            pltpu.SemaphoreType.DMA((64,)),
+            pltpu.SemaphoreType.DMA((Z_SLOTS + 32,)),
             pltpu.SemaphoreType.DMA((12,)),
             pltpu.SemaphoreType.DMA((12,)),
         ],

time: 78.5 us -> 74.5 us (0.949)
  Pallas kernels: 77.7 us -> 73.2 us
    pallas_call x1, Pallas kernels: 37.6 us -> 28.2 us  [scatter(): pl.pallas_call(scatter_kernel, out_shape=jax.ShapeDtypeStruct((ROWS, 2 *...]
    pallas_call x1, Pallas kernels: 7.3 us -> 12.3 us  [attention(): pl.pallas_call(attention_kernel, out_shape=(jax.ShapeDtypeStruct(q.shape,...]
where the time goes in v5:
time: 74.5 us; the launch traced here: 74 us
  Pallas kernels  73.2 us (98%)
    pallas_call x1, Pallas kernels, gather(): pl.pallas_call(gather_kernel, out_shape=(pltpu.VMEM(PIECES, BF16), pltpu....  32.1 us
    pallas_call x1, Pallas kernels, scatter(): pl.pallas_call(scatter_kernel, out_shape=jax.ShapeDtypeStruct((ROWS, 2 *...  28.2 us
    pallas_call x1, Pallas kernels, attention(): pl.pallas_call(attention_kernel, out_shape=(jax.ShapeDtypeStruct(q.shape,...  12.3 us

profile of v5, /device:TPU:32, one launch (start us, length us, event | category | flops | bytes accessed | tf_op | source)
XLA Modules:
  0.0 74.0 jit_solution(10857075585398965989)
XLA Ops:
  0.6 0.0 copy-start
  0.6 0.0 copy-start.1
  0.7 0.0 copy-start.2
  0.7 32.1 %gather.1 = (bf16[4,2,4,2,128,256]{5,4,3,2,1,0:T(8,128)(2,1)S(1)}, bf16[128,1024]{1,0:T(8,128)(2,1)S(1)}) custom-call(bf16[128,128]{1,0:T(8,128)(2,1)} %k_ref.1, bf16[128,128]{1,0:T(8,128)(2,1)} %v_ref.1, bf16[32,4096]{1,0:T(8,128)(2,1)} %da_ref.1, bf16[1024,4096]{1,0:T(8,128)(2,1)} %w_ref.1), custom_call_target="tpu_custom_call" | custom-call | tf_op jit(solution)/shard_map/gather/pallas_call | solution.py:244
  32.8 0.0 copy-done
  32.8 0.0 copy-done.1
  32.8 0.0 copy-done.2
  32.9 12.3 %attention.1 = (bf16[128,1024]{1,0:T(8,128)(2,1)}, bf16[128,1024]{1,0:T(8,128)(2,1)}, bf16[8192,256]{1,0:T(8,128)(2,1)S(1)}) custom-call(s32[1]{0:T(128)} %bitcast.seq_ref, s32[128]{0:T(128)S(1)} %copy-done.2, s32[64,128]{1,0:T(8,128)S(1)} %bitcast.6, bf16[128,1024]{1,0:T(8,128)(2,1)S(1)} %copy-done, bf16[128,1024]{1,0:T(8,128)(2,1)S(1)} %get-tuple-element.11.g_ref, ...), custom_call_target="tpu_custom_call" | custom-call | tf_op jit(solution)/shard_map/attention/pallas_call | solution.py:421
  45.1 28.2 %scatter.1.sum_ref = f32[128,256]{1,0:T(8,128)S(1)} custom-call(bf16[4,2,4,2,128,256]{5,4,3,2,1,0:T(8,128)(2,1)S(1)} %bitcast.5), custom_call_target="tpu_custom_call" | custom-call | tf_op jit(solution)/shard_map/scatter/pallas_call | solution.py:658
  73.3 0.6 finish.1
Async XLA Ops:
  0.6 32.2 %copy-start = (bf16[128,1024]{1,0:T(8,128)(2,1)S(1)}, bf16[128,1024]{1,0:T(8,128)(2,1)}, u32[]{:S(2)}) copy-start(bf16[128,1024]{1,0:T(8,128)(2,1)} %q_ref.1) | copy-start | bytes 786436
  0.6 32.2 %copy-start.1 = (s32[8192]{0:T(1024)S(1)}, s32[8192]{0:T(1024)}, u32[]{:S(2)}) copy-start(s32[8192]{0:T(1024)} %param.10) | copy-start | bytes 98308
  0.7 32.2 %copy-start.2 = (s32[128]{0:T(128)S(1)}, s32[128]{0:T(128)}, u32[]{:S(2)}) copy-start(s32[128]{0:T(128)} %order_ref.1) | copy-start | bytes 1540

commit v6 on v5

--- a/solution.py
+++ b/solution.py
@@ -583,40 +583,38 @@
                 by_z.pass_on(me.dy(i), me.dz(-s), got, down_slot(s, i), down_z)
 
         ready(4)
+        y_far(by_y, 4)
         for i in (0, -1, 1, 2):
             if i in (0, 1):
                 by_z.pass_on(me.dy(i), me.dz(4), (), up_slot(4, i), up_2z)
             else:
                 by_z.pass_on(me.dy(i), me.dz(4), (), down_slot(4, i), down_2z)
-        y_far(by_y, 4)
-        ready(3)
-        ready(-3)
+        for s in (3, -3):
+            ready(s)
+            y_far(by_y, s)
         z_step(3)
-        for s in (3, -3):
+        for s in (2, -2):
+            ready(s)
             y_far(by_y, s)
-        ready(2)
-        ready(-2)
+        for s in (4, 3, -3):
+            y_near(by_y, s)
+        z_step(2)
+        for s in (1, -1, 0):
+            ready(s)
+            y_far(by_y, s)
         for s in (2, -2):
-            y_far(by_y, s)
-        y_near(by_y, 4)
-        z_step(2)
-        ready(1)
-        ready(-1)
-        for s in (1, -1):
-            y_far(by_y, s)
-        for s in (3, -3):
-            y_near(by_y, s)
-        ready(0)
-        y_far(by_y, 0)
-        z_step(1)
-        for s in (2, -2, 1, -1, 0):
             y_near(by_y, s)
         for s in (4, 3, -3):
+            along_z(by_y, s)
+        z_step(1)
+        for s in (1, -1, 0):
+            y_near(by_y, s)
+        for s in (2, -2):
             along_z(by_y, s)
         last = lambda i: (up_slot(1, i), down_slot(1, i))
         for i in (1, -1, 2):
             by_z.pass_on(me.dy(i), z, last(i), 32 + order.index(i), me.device(y=me.dy(i)))
-        for s in (1, -1, 2, -2):
+        for s in (1, -1):
             along_z(by_y, s)
         by_z.terms(y, z, last(0) + (33, 34, 35), write)
         y_last(by_y)
@@ -644,10 +642,14 @@
             y_far(by_y, s)
         ready(1)
         ready(-1)
-        for s in FAR_FIRST:
+        for s in FAR_FIRST[:6]:
             y_near(by_y, s)
         ready(0)
-        for s in FAR_FIRST[:-1]:
+        for s in (4, 3, -3):
+            along_z(by_y, s)
+        for s in FAR_FIRST[6:]:
+            y_near(by_y, s)
+        for s in FAR_FIRST[3:-1]:
             along_z(by_y, s)
         y_last(by_y)
         mate_sends.wait()

time: 74.5 us -> 75.3 us (1.011); the launches traced: 74 us -> 73.8 us
    pallas_call x1, Pallas kernels: 12.3 us -> 8.62 us  [attention(): pl.pallas_call(attention_kernel, out_shape=(jax.ShapeDtypeStruct(q.shape,...]
    pallas_call x1, Pallas kernels: 28.2 us -> 31.7 us  [scatter(): pl.pallas_call(scatter_kernel, out_shape=jax.ShapeDtypeStruct((ROWS, 2 *...]
where the time goes in v6:
time: 75.3 us; the launch traced here: 73.8 us
  Pallas kernels  73.1 us (97%)
    pallas_call x1, Pallas kernels, gather(): pl.pallas_call(gather_kernel, out_shape=(pltpu.VMEM(PIECES, BF16), pltpu....  32.1 us
    pallas_call x1, Pallas kernels, scatter(): pl.pallas_call(scatter_kernel, out_shape=jax.ShapeDtypeStruct((ROWS, 2 *...  31.7 us
    pallas_call x1, Pallas kernels, attention(): pl.pallas_call(attention_kernel, out_shape=(jax.ShapeDtypeStruct(q.shape,...  8.62 us

profile of v6, /device:TPU:32, one launch (start us, length us, event | category | flops | bytes accessed | tf_op | source)
XLA Modules:
  0.0 73.8 jit_solution(16004881332305327809)
XLA Ops:
  0.6 0.0 copy-start
  0.6 0.0 copy-start.1
  0.7 0.0 copy-start.2
  0.7 32.1 %gather.1 = (bf16[4,2,4,2,128,256]{5,4,3,2,1,0:T(8,128)(2,1)S(1)}, bf16[128,1024]{1,0:T(8,128)(2,1)S(1)}) custom-call(bf16[128,128]{1,0:T(8,128)(2,1)} %k_ref.1, bf16[128,128]{1,0:T(8,128)(2,1)} %v_ref.1, bf16[32,4096]{1,0:T(8,128)(2,1)} %da_ref.1, bf16[1024,4096]{1,0:T(8,128)(2,1)} %w_ref.1), custom_call_target="tpu_custom_call" | custom-call | tf_op jit(solution)/shard_map/gather/pallas_call | solution.py:244
  32.8 0.0 copy-done
  32.8 0.0 copy-done.1
  32.8 0.0 copy-done.2
  32.9 8.6 %attention.1 = (bf16[128,1024]{1,0:T(8,128)(2,1)}, bf16[128,1024]{1,0:T(8,128)(2,1)}, bf16[8192,256]{1,0:T(8,128)(2,1)S(1)}) custom-call(s32[1]{0:T(128)} %bitcast.seq_ref, s32[128]{0:T(128)S(1)} %copy-done.2, s32[64,128]{1,0:T(8,128)S(1)} %bitcast.6, bf16[128,1024]{1,0:T(8,128)(2,1)S(1)} %copy-done, bf16[128,1024]{1,0:T(8,128)(2,1)S(1)} %get-tuple-element.11.g_ref, ...), custom_call_target="tpu_custom_call" | custom-call | tf_op jit(solution)/shard_map/attention/pallas_call | solution.py:421
  41.5 31.7 %scatter.1.sum_ref = f32[128,256]{1,0:T(8,128)S(1)} custom-call(bf16[4,2,4,2,128,256]{5,4,3,2,1,0:T(8,128)(2,1)S(1)} %bitcast.5), custom_call_target="tpu_custom_call" | custom-call | tf_op jit(solution)/shard_map/scatter/pallas_call | solution.py:660
  73.2 0.6 finish.1
Async XLA Ops:
  0.6 32.2 %copy-start = (bf16[128,1024]{1,0:T(8,128)(2,1)S(1)}, bf16[128,1024]{1,0:T(8,128)(2,1)}, u32[]{:S(2)}) copy-start(bf16[128,1024]{1,0:T(8,128)(2,1)} %q_ref.1) | copy-start | bytes 786436
  0.6 32.2 %copy-start.1 = (s32[8192]{0:T(1024)S(1)}, s32[8192]{0:T(1024)}, u32[]{:S(2)}) copy-start(s32[8192]{0:T(1024)} %param.10) | copy-start | bytes 98308
  0.7 32.2 %copy-start.2 = (s32[128]{0:T(128)S(1)}, s32[128]{0:T(128)}, u32[]{:S(2)}) copy-start(s32[128]{0:T(128)} %order_ref.1) | copy-start | bytes 1540
